TPU v7x, 256 devices: a whole 4x4x8 slice. The times are simulated.
256 devices in a mesh: pipe: 4 (over x), dp: 16 (over z, core), mp: 4 (over y).
Axes of the slice: x: 4, y: 4, z: 8, core: 2. Of those that a mesh axis runs over, the one named last changes fastest.
Arguments:
- queries: bfloat16 [4, 4, 2048, 8192], P('pipe', None, 'dp', 'mp'), may hold values from -6 to 6
- grad_out: bfloat16 [4, 4, 2048, 8192], P('pipe', None, 'dp', 'mp'), may hold values from -6 to 6
- features: bfloat16 [4, 2048, 8192], P('pipe', 'dp', 'mp'), may hold values from -6 to 6
- w_key: bfloat16 [4, 8192, 1024], P('pipe', ('mp', 'dp')), may hold values from -0.0625 to 0.0625
- w_value: bfloat16 [4, 8192, 1024], P('pipe', ('mp', 'dp')), may hold values from -0.0625 to 0.0625
- q_gain: float32 [4, 128], P('pipe'), may hold values from 0.1 to 1.9
- k_gain: float32 [4, 128], P('pipe'), may hold values from 0.1 to 1.9
- tile_counts: int32 [4, 16, 2], P(None, 'dp'), may hold values from 1 to 4, as said below
- image_starts: int32 [4, 16, 2], P(None, 'dp'), may hold values from 0 to 127, as said below
Outputs:
- feature_grads: bfloat16 [4, 2048, 8192], P('pipe', 'dp', 'mp')
- key_weight_grads: bfloat16 [4, 8192, 1024], P('pipe', ('mp', 'dp'))
- value_weight_grads: bfloat16 [4, 8192, 1024], P('pipe', ('mp', 'dp'))
Inputs may be any that keep to these rules, and one draw needn't show every extreme that they name: `tile_counts`: every image has at least one tile, and some image of some bin has 4 tiles. `image_starts`: within a bin the images' positions never fall.
All inputs are finite; a program needn't handle non-finite values.
Results may differ from a plain program's by a relative error of at most 0.028.
Values may be sent and summed in bfloat16 or wider, within the bound.
A program may use at most 128 MiB of HBM per device.

v0:
```python
import math

import jax
import jax.numpy as jnp
from jax import lax
from jax.sharding import PartitionSpec as P

TILE_TOK = 16


EPSILON = 1e-05


def normed(values, gain):
    inverse = lax.rsqrt(jnp.mean(values * values, axis=-1, keepdims=True) + EPSILON)
    return values * inverse * gain


def visible_slots(tile_counts, image_starts, image_len, text_len):
    lengths = tile_counts * TILE_TOK
    image_upper = jnp.cumsum(lengths, axis=-1)
    image_lower = image_upper - lengths
    slot_index = jnp.arange(image_len, dtype=jnp.int32)
    text_index = jnp.arange(text_len, dtype=jnp.int32)
    inside = (
        (slot_index >= image_lower[..., None]) & (slot_index < image_upper[..., None])
    ).astype(jnp.float32)
    text_after = (text_index >= image_starts[..., None]).astype(jnp.float32)
    return jnp.einsum("...ij,...it->...jt", inside, text_after)


def attention_grads(query, grad_out, key_pre, value_rounded, visible, q_gain, k_gain):
    root_scale = 1.0 / math.sqrt(query.shape[-1])
    query_normed = normed(query.astype(jnp.float32), q_gain).astype(jnp.bfloat16)
    key_normed = normed(key_pre, k_gain).astype(jnp.bfloat16)
    scores = (
        jnp.einsum(
            "bjgd,btghd->bghjt", key_normed, query_normed, preferred_element_type=jnp.float32
        )
        * root_scale
    )
    weights = jnp.exp(scores) * visible[:, None, None]
    denominator = jnp.sum(weights, axis=3, keepdims=True)
    probability = weights / jnp.where(denominator > 0, denominator, 1.0)
    prob_rounded = probability.astype(jnp.bfloat16)
    value_grad = jnp.einsum(
        "bghjt,btghd->bjgd", prob_rounded, grad_out, preferred_element_type=jnp.float32
    ).astype(jnp.bfloat16)
    prob_grad = jnp.einsum(
        "btghd,bjgd->bghjt", grad_out, value_rounded, preferred_element_type=jnp.float32
    )
    row_delta = jnp.sum(probability * prob_grad, axis=3, keepdims=True)
    score_grad = (probability * (prob_grad - row_delta)).astype(jnp.bfloat16)
    normed_grad = (
        jnp.einsum(
            "bghjt,btghd->bjgd", score_grad, query_normed, preferred_element_type=jnp.float32
        )
        * root_scale
    )
    inverse = lax.rsqrt(jnp.mean(key_pre * key_pre, axis=-1, keepdims=True) + EPSILON)
    scaled = normed_grad * k_gain
    key_grad = inverse * scaled - key_pre * inverse**3 * jnp.mean(
        scaled * key_pre, axis=-1, keepdims=True
    )
    return (key_grad.astype(jnp.bfloat16), value_grad)


def per_device(
    queries, grad_out, features, w_key, w_value, q_gain, k_gain, tile_counts, image_starts
):
    head_dim = q_gain.shape[1]
    features_all = lax.all_gather(features, "pipe", axis=0, tiled=True)
    micro_count, image_len, quarter = features_all.shape
    slot_rows = micro_count * image_len
    flattened = features_all.reshape(slot_rows, quarter)
    weight_pair = lax.all_gather(jnp.stack([w_key[0], w_value[0]]), "dp", axis=1, tiled=True)
    partial_kv = jnp.einsum(
        "bi,sik->bsk", flattened, weight_pair, preferred_element_type=jnp.float32
    )
    summed_kv = lax.psum_scatter(
        partial_kv.astype(jnp.bfloat16), "mp", scatter_dimension=2, tiled=True
    ).astype(jnp.float32)
    local_width = summed_kv.shape[2]
    key_heads = local_width // head_dim
    query_local = queries[0]
    text_len = query_local.shape[1]
    groups = query_local.shape[2] // local_width
    shape_q = (micro_count, text_len, key_heads, groups, head_dim)
    shape_k = (micro_count, image_len, key_heads, head_dim)
    visible = visible_slots(tile_counts[:, 0], image_starts[:, 0], image_len, text_len)
    key_grad, value_grad = attention_grads(
        query_local.reshape(shape_q),
        grad_out[0].reshape(shape_q),
        summed_kv[:, 0].reshape(shape_k),
        summed_kv[:, 1].astype(jnp.bfloat16).reshape(shape_k),
        visible,
        q_gain[0],
        k_gain[0],
    )
    local_grads = jnp.stack(
        [key_grad.reshape(slot_rows, local_width), value_grad.reshape(slot_rows, local_width)],
        axis=1,
    )
    kv_grads = lax.all_gather(local_grads, "mp", axis=2, tiled=True)
    image_grads = lax.psum_scatter(
        jnp.einsum("bsk,sik->bi", kv_grads, weight_pair, preferred_element_type=jnp.float32).astype(
            jnp.bfloat16
        ),
        "pipe",
        scatter_dimension=0,
        tiled=True,
    ).astype(jnp.float32)
    dp_count = lax.axis_size("dp")
    factor = 1.0 / (micro_count * dp_count)
    summed = lax.psum_scatter(
        jnp.einsum("bi,bsk->isk", flattened, kv_grads, preferred_element_type=jnp.float32).astype(
            jnp.bfloat16
        ),
        "dp",
        scatter_dimension=0,
        tiled=True,
    ).astype(jnp.float32)
    scaled_grads = (summed * factor).astype(jnp.bfloat16)
    return (
        image_grads.reshape(1, image_len, quarter).astype(jnp.bfloat16),
        scaled_grads[:, 0][None],
        scaled_grads[:, 1][None],
    )


def solution(mesh):
    in_specs = (
        P("pipe", None, "dp", "mp"),
        P("pipe", None, "dp", "mp"),
        P("pipe", "dp", "mp"),
        P("pipe", ("mp", "dp"), None),
        P("pipe", ("mp", "dp"), None),
        P("pipe", None),
        P("pipe", None),
        P(None, "dp", None),
        P(None, "dp", None),
    )
    out_specs = (
        P("pipe", "dp", "mp"),
        P("pipe", ("mp", "dp"), None),
        P("pipe", ("mp", "dp"), None),
    )
    return jax.shard_map(
        per_device, mesh=mesh, in_specs=in_specs, out_specs=out_specs, check_vma=False
    )
```

profile of v0, /device:TPU:1, one launch (start us, length us, event | category | flops | bytes accessed | tf_op | source)
XLA Modules:
  0.0 346.6 jit_solution(14263636913077955030)
XLA Ops:
  7.2 0.0 all-gather.6.cloned.1.call-start
  7.2 0.7 all-gather.6.cloned.1.call-update
  7.9 0.0 all-gather.4.cloned.1.call-start
  7.9 1.1 copy.99
  9.1 1.1 copy.98
  10.2 0.8 pad_maximum_fusion
  11.0 0.0 all-gather.4.cloned.1.call-update
  11.1 0.0 reduce-scatter.6.cloned.1.call-start
  11.1 35.9 %all-gather.6.cloned.1.call-done = bf16[4,128,2048]{2,1,0:T(8,128)(2,1)} async-done(((bf16[1,128,2048]{2,1,0:T(8,128)(2,1)}), bf16[4,128,2048]{2,1,0:T(8,128)(2,1)}) %all-gather.6.cloned.1.call-update) | async-done | bytes 2097168 | tf_op jit(solution)/shard_map/all_gather | solution.py:72
  47.0 69.0 %all-gather.4.cloned.1.call-done = bf16[2,2048,1024]{1,2,0:T(8,128)(2,1)} async-done(((bf16[2,128,1024]{1,2,0:T(8,128)(2,1)}), bf16[2,2048,1024]{1,2,0:T(8,128)(2,1)}) %all-gather.4.cloned.1.call-update) | async-done | bytes 8388624 | tf_op jit(solution)/shard_map/all_gather | solution.py:76
  116.0 9.9 %convert_bitcast_fusion = bf16[512,2,1024]{0,2,1:T(8,128)(2,1)} fusion(bf16[2,2048,1024]{1,2,0:T(8,128)(2,1)} %all-gather.4.cloned.1.call-done, bf16[512,2048,1]{1,0,2:T(8,128)(2,1)} %bitcast.111), kind=kOutput, calls=%fused_computation.18 | convolution fusion | flops 4296015872 | bytes 12582912 | tf_op jit(solution)/shard_map/bi,sik->bsk/dot_general | solution.py:77
  125.9 0.0 reduce-scatter.6.cloned.1.call-update
  125.9 0.2 all-gather.8.cloned.1.call-start
  126.1 2.2 copy.140
  128.3 0.1 copy.108
  128.5 0.1 copy.107
  128.6 0.1 copy.106
  128.7 2.2 copy.139
  130.9 0.0 copy-start.8
  130.9 0.0 copy-start.6
  130.9 1.9 copy-done
  132.8 1.7 multiply_reduce_fusion
  134.5 0.2 copy.101
  134.7 0.2 copy.102
  135.0 1.0 fusion.44
  136.0 3.8 %multiply_convert_fusion = bf16[4,128,2,8,128]{4,3,2,1,0:T(8,128)(2,1)} fusion(f32[4,128,2,8,128]{4,3,2,1,0:T(8,128)} %bitcast.101, f32[128]{0:T(128)S(1)} %bitcast.110, f32[4,128,2,8]{3,2,1,0:T(2,128)S(1)} %copy.102), kind=kLoop, calls=%fused_computation.8 | loop fusion | flops 3145728 | bytes 6324736 | tf_op jit(solution)/shard_map/convert_element_type | solution.py:34
  139.8 14.8 %reduce-scatter.6.cloned.1.call-done = bf16[512,2,256]{0,2,1:T(8,128)(2,1)} async-done(((bf16[512,2,1024]{0,2,1:T(8,128)(2,1)}), bf16[512,2,256]{0,2,1:T(8,128)(2,1)}) %reduce-scatter.6.cloned.1.call-update) | async-done | bytes 524304 | tf_op jit(solution)/shard_map/reduce_scatter | solution.py:80
  154.6 1.1 fusion.58
  155.7 0.2 reshape.65
  155.9 0.0 copy-start.2
  155.9 0.1 multiply_reduce_fusion.2
  156.1 3.0 fusion.4
  159.1 1.3 fusion.34
  160.5 0.6 copy-done.9
  161.1 0.3 copy.120
  161.3 0.2 stack_reshape.7
  161.5 0.1 convert_element_type.71
  161.6 0.0 copy-start.3
  161.6 0.8 fusion.13
  162.4 0.2 copy-done.3
  162.5 1.3 copy-done.10
  163.9 2.5 fusion.2
  166.4 4.4 %copy.112 = bf16[4,2,8,128,128]{3,2,4,1,0:T(8,128)(2,1)} copy(bf16[4,2,8,128,128]{4,3,2,1,0:T(8,128)(2,1)} %fusion.2) | data formatting | bytes 4194304 | tf_op jit(solution)/shard_map/convert_element_type | solution.py:53
  170.8 2.4 multiply_reduce_fusion.1
  173.3 0.1 subtract_convert_fusion
  173.4 0.2 copy.118
  173.6 0.2 stack_reshape.6
  173.8 0.8 pad_maximum_fusion.1
  174.6 0.0 all-gather.8.cloned.1.call-update
  174.6 0.3 reduce-scatter.10.cloned.1.call-start
  174.9 35.6 %all-gather.8.cloned.1.call-done = bf16[512,2,1024]{2,0,1:T(8,128)(2,1)} async-done(((bf16[512,2,256]{2,0,1:T(8,128)(2,1)}), bf16[512,2,1024]{2,0,1:T(8,128)(2,1)}) %all-gather.8.cloned.1.call-update) | async-done | bytes 2097168 | tf_op jit(solution)/shard_map/all_gather | solution.py:104
  210.5 10.0 %convolution_convert_fusion = bf16[2,1024,2048]{2,1,0:T(8,128)(2,1)} fusion(bf16[512,2,1024]{2,0,1:T(8,128)(2,1)} %all-gather.8.cloned.1.call-done, bf16[512,2048,1]{1,0,2:T(8,128)(2,1)} %bitcast.112), kind=kOutput, calls=%fused_computation.1 | convolution fusion | flops 4299161600 | bytes 12582912 | tf_op jit(solution)/shard_map/bi,bsk->isk/dot_general | solution.py:116
  220.6 12.4 %copy.137 = bf16[2048,2048]{1,0:T(8,128)(2,1)} copy(bf16[2048,2048]{0,1:T(8,128)(2,1)} %bitcast.104) | data formatting | bytes 16777216
  232.9 0.0 reduce-scatter.10.cloned.1.call-update
  233.0 0.0 reduce-scatter.8.cloned.1.call-start
  233.0 1.5 copy-done.7
  234.5 9.1 %bitcast_convert_fusion = bf16[512,2048]{1,0:T(8,128)(2,1)} fusion(bf16[512,2,1024]{2,0,1:T(8,128)(2,1)S(1)} %copy-done.7, bf16[2,2048,1024]{1,2,0:T(8,128)(2,1)} %all-gather.4.cloned.1.call-done), kind=kOutput, calls=%fused_computation.2 | convolution fusion | flops 4296015872 | bytes 12582912 | tf_op jit(solution)/shard_map/bsk,sik->bi/dot_general | solution.py:106
  243.6 0.0 reduce-scatter.8.cloned.1.call-update
  243.6 59.0 %reduce-scatter.10.cloned.1.call-done = bf16[128,2048]{1,0:T(8,128)(2,1)} async-done(((bf16[2048,2048]{1,0:T(8,128)(2,1)}), bf16[128,2048]{1,0:T(8,128)(2,1)}) %reduce-scatter.10.cloned.1.call-update) | async-done | bytes 524304
  302.6 1.3 copy.138
  303.9 0.1 multiply_convert_fusion.1
  304.1 0.9 copy.123
  304.9 0.8 copy.124
  305.8 34.0 %reduce-scatter.8.cloned.1.call-done = bf16[128,2048]{1,0:T(8,128)(2,1)} async-done(((bf16[512,2048]{1,0:T(8,128)(2,1)}), bf16[128,2048]{1,0:T(8,128)(2,1)}) %reduce-scatter.8.cloned.1.call-update) | async-done | bytes 524304 | tf_op jit(solution)/shard_map/reduce_scatter | solution.py:105
  (25 shorter events, 0.2 us)
Async XLA Ops:
  7.2 39.8 %all-gather.6.cloned.1.call-start = ((), (), s32[]{:S(2)}) async-start(), calls=%async_computation.4 | async-start | bytes 2621440 | tf_op jit(solution)/shard_map/all_gather | solution.py:72
  7.9 108.1 %all-gather.4.cloned.1.call-start = ((), (), s32[]{:S(2)}) async-start(), calls=%async_computation.3 | async-start | bytes 8912896 | tf_op jit(solution)/shard_map/all_gather | solution.py:76
  11.1 143.5 %reduce-scatter.6.cloned.1.call-start = ((), (), s32[]{:S(2)}) async-start(), calls=%async_computation.5 | async-start | bytes 2621440 | tf_op jit(solution)/shard_map/reduce_scatter | solution.py:80
  125.9 2.5 copy-start.5
  125.9 2.6 copy-start.4
  125.9 84.6 %all-gather.8.cloned.1.call-start = ((), (), s32[]{:S(2)}) async-start(), calls=%async_computation.6 | async-start | bytes 2621440 | tf_op jit(solution)/shard_map/all_gather | solution.py:104
  130.9 2.0 copy-start
  130.9 4.1 %copy-start.8 = (f32[1,128]{1,0:T(1,128)S(1)}, f32[1,128]{1,0:T(1,128)}, u32[]{:S(2)}) copy-start(f32[1,128]{1,0:T(1,128)} %param.15) | copy-start | bytes 1540
  130.9 5.1 %copy-start.6 = (f32[1,128]{1,0:T(1,128)S(1)}, f32[1,128]{1,0:T(1,128)}, u32[]{:S(2)}) copy-start(f32[1,128]{1,0:T(1,128)} %param.14) | copy-start | bytes 1540
  155.9 3.3 copy-start.2
  159.1 2.0 copy-start.9
  161.6 1.0 copy-start.3
  161.6 2.3 copy-start.10
  166.4 4.4 %copy-start.1 = (bf16[4,128,2,8,128]{4,3,2,1,0:T(8,128)(2,1)S(1)}, bf16[4,128,2,8,128]{4,3,2,1,0:T(8,128)(2,1)}, u32[]{:S(2)}) copy-start(bf16[4,128,2,8,128]{4,3,2,1,0:T(8,128)(2,1)} %multiply_convert_fusion) | copy-start | bytes 6291460
  174.6 128.0 %reduce-scatter.10.cloned.1.call-start = ((), (), s32[]{:S(2)}) async-start(), calls=%async_computation.8 | async-start | bytes 8912896
  232.9 1.6 copy-start.7
  233.0 106.8 %reduce-scatter.8.cloned.1.call-start = ((), (), s32[]{:S(2)}) async-start(), calls=%async_computation.7 | async-start | bytes 2621440 | tf_op jit(solution)/shard_map/reduce_scatter | solution.py:105
Sparse Core Ops, SparseCore 0:
  9.8 37.1 all-gather.5
  49.3 66.6 all-gather.3
  126.0 28.5 reduce-scatter.5
  174.8 35.7 all-gather.7
  233.1 69.4 reduce-scatter.9
  305.7 33.9 reduce-scatter.7
where the time goes:
time: 347 us
  waiting for transfers between devices  249 us (72%)
  matrix products  37.6 us (11%)
  local copies, waits for them, and re-layouts  33.8 us (10%)
  between operations  14.4 us (4%)
  other arithmetic  11.2 us (3%)
    all_gather x1, waiting for transfers between devices, per_device(): lax.all_gather(jnp.stack([w_key[0], w_value[0]]), 'dp', axis=1, tiled=True)  69 us
    unnamed x7, waiting for transfers between devices  59.7 us
    all_gather x1, waiting for transfers between devices, per_device(): features_all = lax.all_gather(features, 'pipe', axis=0, tiled=True)  35.9 us
    all_gather x1, waiting for transfers between devices, per_device(): kv_grads = lax.all_gather(local_grads, 'mp', axis=2, tiled=True)  35.6 us
    reduce_scatter x1, waiting for transfers between devices, per_device(): lax.psum_scatter(jnp.einsum('bsk,sik->bi', kv_grads, weight_pair, preferr...  34 us
    unnamed x30, local copies, waits for them, and re-layouts  27.6 us
    reduce_scatter x1, waiting for transfers between devices, per_device(): lax.psum_scatter(partial_kv.astype(jnp.bfloat16), 'mp', scatter_dimension...  14.8 us
    dot_general x1, matrix products, per_device(): jnp.einsum('bi,bsk->isk', flattened, kv_grads, preferred_element_type=jnp...  10 us
  transfers between devices with their start and end apart: 6, of which 6 were waited for; matrix products, arithmetic and copies ran while one was open for 8% of the time, Pallas kernels for 0%

commit v1 on v0

v1 whole, which is shorter than its diff:
```python
import math

import jax
import jax.numpy as jnp
from jax import lax
from jax.experimental import pallas as pl
from jax.experimental.pallas import tpu as pltpu
from jax.sharding import PartitionSpec as P

TILE_TOK = 16
EPSILON = 1e-05
NX, NY, NZ = 4, 4, 8
HD = 128
ROWS = 128
WIDTH = 2048
GROUPS = 8
OFFSETS = (0, 1, 3, 2)
RIGHT, LEFT = 0, 1
HALF = NZ // 2
BF = jnp.bfloat16
F32 = jnp.float32
MESH = pl.DeviceIdType.MESH
N_SEMS = 224
NT = (((1,), (1,)), ((), ()))


def kernel(
    queries,
    grad_out,
    features,
    w_key,
    w_value,
    q_gain,
    k_gain,
    tiles,
    starts,
    out_f,
    out_k,
    out_v,
    qb,
    do,
    fa,
    ft,
    wb,
    ps,
    rk,
    gs,
    ga,
    pw,
    sb,
    rb,
    osd,
    ow,
    ds,
    dr,
    dk,
    dx,
    xr,
    send_sems,
    recv_sems,
    local_sems,
):
    px = lax.axis_index("pipe")
    dd = lax.axis_index("dp")
    qy = lax.axis_index("mp")
    zz = dd // 2
    cc = dd % 2
    oc = 1 - cc
    kinds = (w_key, w_value)

    def at_x(step):
        return ((px + step) % NX, dd, qy)

    def at_y(step, core):
        return (px, zz * 2 + core, (qy + step) % NY)

    def at_z(step):
        return (px, ((zz + step) % NZ) * 2 + cc, qy)

    sibling = (px, zz * 2 + oc, qy)

    ids = {}
    started = []

    def sem_of(key):
        return ids.setdefault(key, len(ids))

    def remote(key, src, dst, device):
        n = sem_of(key)
        return pltpu.make_async_remote_copy(
            src_ref=src,
            dst_ref=dst,
            send_sem=send_sems.at[n],
            recv_sem=recv_sems.at[n],
            device_id=device,
            device_id_type=MESH,
        )

    def send(key, src, dst, device):
        copy = remote(key, src, dst, device)
        copy.start()
        started.append(copy)

    def receive(key, dst):
        remote(key, dst, dst, sibling).wait_recv()

    local_ids = {}

    def local(key, src, dst):
        n = local_ids.setdefault(key, len(local_ids))
        return pltpu.make_async_copy(src, dst, local_sems.at[n])

    barrier = pltpu.get_barrier_semaphore()
    partners = [sibling, at_z(1), at_z(NZ - 1)]
    partners += [at_x(step) for step in (1, 2, 3)]
    partners += [at_y(step, core) for step in (1, 2, 3) for core in (cc, oc)]
    for device in partners:
        pl.semaphore_signal(barrier, inc=1, device_id=device, device_id_type=MESH)

    def weight_columns(ref, hh, j):
        return ref.at[0, :, pl.ds((2 * j + hh) * HD, HD)]

    for kind in (0, 1):

        @pl.when(cc == kind)
        def _():
            for hh in (0, 1):
                for j in range(NY):
                    local(
                        ("w", hh, j),
                        weight_columns(kinds[kind], hh, j),
                        wb.at[hh, zz, cc, :, pl.ds(j * HD, HD)],
                    ).start()

    local("f", features.at[0], fa.at[0, cc]).start()
    for slot in range(NX):
        local(("q", slot), queries.at[0, (px + OFFSETS[slot]) % NX], qb.at[slot]).start()
        local(("d", slot), grad_out.at[0, (px + OFFSETS[slot]) % NX], do.at[slot]).start()

    pl.semaphore_wait(barrier, len(partners))

    for kind in (0, 1):

        @pl.when(oc == kind)
        def _():
            for hh in (0, 1):
                for j in range(NY):
                    remote(
                        ("w", hh, j),
                        weight_columns(kinds[kind], hh, j),
                        wb.at[hh, zz, cc, :, pl.ds(j * HD, HD)],
                        sibling,
                    ).start()

    for hh in (0, 1):
        for j in range(NY):
            piece = wb.at[hh, zz, cc, :, pl.ds(j * HD, HD)]
            started.append(remote(("w", hh, j), piece, piece, sibling))

    send(("fx", 3), features.at[0], fa.at[2, cc], at_x(1))
    send(("fx", 1), features.at[0], fa.at[1, cc], at_x(3))
    send(("fs", 0), features.at[0], fa.at[0, cc], sibling)

    def gather_pieces(direction, k):
        if k == HALF - 1:
            return (direction,)
        return (0, 1)

    def origin(direction, k):
        return (zz - k + NZ) % NZ if direction == RIGHT else (zz + k) % NZ

    def gather_send(hh, k, pieces=(0, 1)):
        for piece in pieces:
            for direction in (RIGHT, LEFT):
                if piece not in gather_pieces(direction, k):
                    continue
                block = wb.at[hh, origin(direction, k), piece]
                if k:
                    receive(("ag", direction, hh, k - 1, piece), block)
                send(
                    ("ag", direction, hh, k, piece),
                    block,
                    block,
                    at_z(1 if direction == RIGHT else NZ - 1),
                )

    def gather_rest(hh):
        for direction in (RIGHT, LEFT):
            piece = 1 - direction
            receive(
                ("ag", direction, hh, HALF - 2, piece),
                wb.at[hh, origin(direction, HALF - 1), piece],
            )

    def gather_last(hh):
        for direction in (RIGHT, LEFT):
            receive(
                ("ag", direction, hh, HALF - 1, direction),
                wb.at[hh, origin(direction, HALF), direction],
            )

    def own_weights(hh):
        for j in range(NY):
            piece = wb.at[hh, zz, cc, :, pl.ds(j * HD, HD)]
            local(("w", hh, j), piece, piece).wait()
        for j in range(NY):
            piece = wb.at[hh, zz, oc, :, pl.ds(j * HD, HD)]
            receive(("w", hh, j), piece)

    def norm_queries(slot):
        local(("q", slot), qb.at[slot], qb.at[slot]).wait()
        gain = q_gain[...]

        def body(i, carry):
            for u in range(4):
                columns = pl.ds(pl.multiple_of((i * 4 + u) * HD, HD), HD)
                values = qb[slot, :, columns].astype(F32)
                inverse = lax.rsqrt(
                    jnp.mean(values * values, axis=-1, keepdims=True) + EPSILON
                )
                qb[slot, :, columns] = (values * inverse * gain).astype(BF)
            return carry

        lax.fori_loop(0, WIDTH // HD // 4, body, 0)

    def transpose_features(slot, replica):
        place = pl.multiple_of((slot * 2 + replica) * ROWS, ROWS)

        def body(i, carry):
            for u in range(2):
                columns = pl.ds(pl.multiple_of((i * 2 + u) * HD, HD), HD)
                ft[columns, pl.ds(place, ROWS)] = fa[slot, replica, :, columns].T
            return carry

        lax.fori_loop(0, WIDTH // HD // 2, body, 0)

    def project(hh, mg):
        def body(n, carry):
            rows = fa[2 * mg : 2 * mg + 2].reshape(4 * ROWS, WIDTH)
            columns = pl.ds(pl.multiple_of(n * 256, 256), 256)
            weights = wb[hh, :, :, :, columns].reshape(WIDTH, 256)
            total = jnp.dot(rows, weights, preferred_element_type=F32).astype(BF)
            for slot in (0, 1):
                for replica in (0, 1):
                    low = (slot * 2 + replica) * ROWS
                    for j in (0, 1):
                        ps[hh, replica, n * 2 + j, 2 * mg + slot] = total[
                            low : low + ROWS, j * HD : (j + 1) * HD
                        ]
            return carry

        lax.fori_loop(0, 2, body, 0)
        pair = pl.ds(2 * mg, 2)
        for step in (2, 1, 3, 0):
            target = (qy + step) % NY
            for same in (1, 0):
                core = cc if same else oc
                src = ps.at[hh, core, target, pair]
                dst = rk.at[hh, cc, step, pair]
                if step == 0 and same:
                    local(("kv", hh, mg), src, dst).start()
                else:
                    send(("kv", hh, mg, step, same), src, dst, at_y(step, core))

    def projected(hh, mg):
        pair = pl.ds(2 * mg, 2)
        for step in range(NY):
            for same in (1, 0):
                dst = rk.at[hh, cc if same else oc, step, pair]
                if step == 0 and same:
                    local(("kv", hh, mg), dst, dst).wait()
                else:
                    receive(("kv", hh, mg, step, same), dst)

    root_scale = 1.0 / math.sqrt(HD)

    def attend(hh, mg):
        gain = k_gain[...]

        def body(i, carry):
            slot = 2 * mg + i
            micro = (px + i) % NX if mg == 0 else (px + 3 - i) % NX
            key_pre = rk[hh, 0, 0, slot].astype(F32)
            value = rk[hh, 1, 0, slot].astype(F32)
            for step in range(1, NY):
                key_pre += rk[hh, 0, step, slot].astype(F32)
                value += rk[hh, 1, step, slot].astype(F32)
            value = value.astype(BF)
            inverse = lax.rsqrt(
                jnp.mean(key_pre * key_pre, axis=-1, keepdims=True) + EPSILON
            )
            key = (key_pre * inverse * gain).astype(BF)
            slots = lax.broadcasted_iota(jnp.int32, (ROWS, 2 * ROWS), 0)
            texts = lax.broadcasted_iota(jnp.int32, (ROWS, 2 * ROWS), 1) % ROWS
            first = tiles[micro, 0, 0] * TILE_TOK
            second = first + tiles[micro, 0, 1] * TILE_TOK
            seen = ((slots < first) & (texts >= starts[micro, 0, 0])) | (
                (slots >= first) & (slots < second) & (texts >= starts[micro, 0, 1])
            )
            visible = jnp.where(seen, 1.0, 0.0).astype(F32)
            value_grad = jnp.zeros((ROWS, HD), F32)
            normed_grad = jnp.zeros((ROWS, HD), F32)
            for g in range(0, GROUPS, 2):
                low = (hh * GROUPS + g) * HD
                query = jnp.concatenate(
                    [qb[slot, :, low : low + HD], qb[slot, :, low + HD : low + 2 * HD]], axis=0
                )
                grad = jnp.concatenate(
                    [do[slot, :, low : low + HD], do[slot, :, low + HD : low + 2 * HD]], axis=0
                )
                scores = (
                    lax.dot_general(key, query, NT, preferred_element_type=F32) * root_scale
                )
                weights = jnp.exp(scores) * visible
                total = jnp.sum(weights, axis=0, keepdims=True)
                probability = weights * (1.0 / jnp.where(total > 0, total, 1.0))
                prob_grad = lax.dot_general(value, grad, NT, preferred_element_type=F32)
                delta = jnp.sum(probability * prob_grad, axis=0, keepdims=True)
                score_grad = (probability * (prob_grad - delta)).astype(BF)
                value_grad += jnp.dot(
                    probability.astype(BF), grad, preferred_element_type=F32
                )
                normed_grad += jnp.dot(score_grad, query, preferred_element_type=F32)
            scaled = normed_grad * root_scale * gain
            key_grad = inverse * scaled - key_pre * (inverse * inverse * inverse) * jnp.mean(
                scaled * key_pre, axis=-1, keepdims=True
            )
            gs[hh, 0, slot] = key_grad.astype(BF)
            gs[hh, 1, slot] = value_grad.astype(BF)
            return carry

        lax.fori_loop(0, 2, body, 0)
        pair = pl.ds(2 * mg, 2)
        for step in (2, 1, 3, 0):
            for same in (1, 0):
                kind = cc if same else oc
                src = gs.at[hh, kind, pair]
                dst = ga.at[hh, qy, pair, cc]
                if step == 0 and same:
                    local(("g", hh, mg), src, dst).start()
                else:
                    send(("g", hh, mg, step, same), src, dst, at_y(step, kind))

    def gathered(hh, mg):
        pair = pl.ds(2 * mg, 2)
        for step in range(NY):
            source = (qy - step + NY) % NY
            for same in (1, 0):
                dst = ga.at[hh, source, pair, cc if same else oc]
                if step == 0 and same:
                    local(("g", hh, mg), dst, dst).wait()
                else:
                    receive(("g", hh, mg, step, same), dst)

    def weight_term(hh, distance):
        block = (zz + distance) % NZ
        lhs = ft[pl.ds(pl.multiple_of(block * 256, 256), 256), :]

        def body(n, carry):
            columns = pl.ds(pl.multiple_of(n * 256, 256), 256)
            grads = jnp.concatenate(
                [ga[hh, n * 2 + j].reshape(8 * ROWS, HD) for j in (0, 1)], axis=1
            )
            pw[distance, :, columns] = jnp.dot(lhs, grads, preferred_element_type=F32)
            return carry

        lax.fori_loop(0, 2, body, 0)

    def scatter_pieces(direction, k):
        return (direction,) if k == 0 else (0, 1)

    def scatter_send(hh, k, pieces=(0, 1)):
        for piece in pieces:
            for direction in (RIGHT, LEFT):
                if piece not in scatter_pieces(direction, k):
                    continue
                distance = HALF - k if direction == RIGHT else HALF + k
                total = pw[distance, piece * ROWS : (piece + 1) * ROWS, :]
                if k and piece in scatter_pieces(direction, k - 1):
                    arrived = rb.at[hh, direction, k - 1, piece]
                    receive(("rs", direction, hh, k - 1, piece), arrived)
                    total = total + arrived[...].astype(F32)
                sb[hh, direction, k, piece] = total.astype(BF)
                send(
                    ("rs", direction, hh, k, piece),
                    sb.at[hh, direction, k, piece],
                    rb.at[hh, direction, k, piece],
                    at_z(1 if direction == RIGHT else NZ - 1),
                )

    factor = 1.0 / (NX * NZ * 2)

    def scatter_last(hh):
        for direction in (RIGHT, LEFT):
            for piece in (0, 1):
                receive(
                    ("rs", direction, hh, HALF - 1, piece), rb.at[hh, direction, HALF - 1, piece]
                )

        def finished(piece):
            total = (
                pw[0, pl.ds(pl.multiple_of(piece * ROWS, ROWS), ROWS), :]
                + rb[hh, RIGHT, HALF - 1, piece].astype(F32)
                + rb[hh, LEFT, HALF - 1, piece].astype(F32)
            )
            return (total * factor).astype(BF)

        other = finished(oc)
        for j in range(NY):
            osd[hh, j] = other[:, j * HD : (j + 1) * HD]
        send(("ow", hh), osd.at[hh], ow.at[cc, hh], sibling)
        own = finished(cc)
        for j in range(NY):
            ow[cc, hh, j] = own[:, j * HD : (j + 1) * HD]

    def feature_term(slot):
        def body(n, carry):
            columns = pl.ds(pl.multiple_of(n * 256, 256), 256)
            total = jnp.zeros((2 * ROWS, 256), F32)
            for hh in (0, 1):
                grads = jnp.concatenate(
                    [ga[hh, j, slot].reshape(2 * ROWS, HD) for j in range(NY)], axis=1
                )
                weights = wb[hh, n].reshape(256, NY * HD)
                total += lax.dot_general(grads, weights, NT, preferred_element_type=F32)
            pieces = (total[:ROWS], total[ROWS:])
            mine = jnp.where(cc == 0, pieces[0], pieces[1])
            others = jnp.where(cc == 0, pieces[1], pieces[0])
            dk[slot, :, columns] = mine
            ds[slot, :, columns] = others.astype(BF)
            return carry

        lax.fori_loop(0, NZ, body, 0)
        send(("df", slot), ds.at[slot], dr.at[slot], sibling)

    def feature_send(slot):
        receive(("df", slot), dr.at[slot])
        dx[slot] = (dk[slot] + dr[slot].astype(F32)).astype(BF)
        send(("dx", slot), dx.at[slot], xr.at[slot], at_x(OFFSETS[slot]))

    own_weights(0)
    gather_send(0, 0)
    for slot in range(NX):
        norm_queries(slot)
    local("f", fa.at[0, cc], fa.at[0, cc]).wait()
    transpose_features(0, cc)
    gather_send(0, 1, (0,))
    receive(("fs", 0), fa.at[0, oc])
    transpose_features(0, oc)
    gather_send(0, 1, (1,))
    gather_send(0, 2, (0,))
    receive(("fx", 1), fa.at[1, cc])
    send(("fh", 0), fa.at[1, cc, pl.ds(0, 64)], fa.at[3, cc, pl.ds(0, 64)], at_x(3))
    receive(("fx", 3), fa.at[2, cc])
    send(("fh", 1), fa.at[2, cc, pl.ds(64, 64)], fa.at[3, cc, pl.ds(64, 64)], at_x(1))
    send(("fs", 1), fa.at[1, cc], fa.at[1, cc], sibling)
    send(("fs", 2), fa.at[2, cc], fa.at[2, cc], sibling)
    gather_send(0, 2, (1,))
    transpose_features(1, cc)
    transpose_features(2, cc)
    gather_send(0, 3)
    gather_rest(0)
    own_weights(1)
    gather_send(1, 0)
    receive(("fh", 0), fa.at[3, cc, pl.ds(0, 64)])
    receive(("fh", 1), fa.at[3, cc, pl.ds(64, 64)])
    send(("fs", 3), fa.at[3, cc], fa.at[3, cc], sibling)
    gather_last(0)
    receive(("fs", 1), fa.at[1, oc])
    project(0, 0)
    gather_send(1, 1, (0,))
    receive(("fs", 2), fa.at[2, oc])
    receive(("fs", 3), fa.at[3, oc])
    project(0, 1)
    gather_send(1, 1, (1,))
    transpose_features(1, oc)
    transpose_features(2, oc)
    transpose_features(3, cc)
    transpose_features(3, oc)
    for slot in range(NX):
        local(("d", slot), do.at[slot], do.at[slot]).wait()
    gather_send(1, 2, (0,))
    projected(0, 0)
    attend(0, 0)
    gather_send(1, 2, (1,))
    projected(0, 1)
    attend(0, 1)
    gather_send(1, 3)
    gather_rest(1)
    gather_last(1)
    project(1, 0)
    project(1, 1)
    gathered(0, 0)
    gathered(0, 1)
    weight_term(0, HALF)
    scatter_send(0, 0)
    for distance in (3, 5, 2, 6):
        weight_term(0, distance)
    scatter_send(0, 1)
    for distance in (1, 7, 0):
        weight_term(0, distance)
    projected(1, 0)
    attend(1, 0)
    scatter_send(0, 2)
    projected(1, 1)
    attend(1, 1)
    scatter_send(0, 3)
    scatter_last(0)
    gathered(1, 0)
    gathered(1, 1)
    weight_term(1, HALF)
    scatter_send(1, 0)
    for distance in (3, 5):
        weight_term(1, distance)
    feature_term(3)
    scatter_send(1, 1)
    feature_term(1)
    feature_send(3)
    for distance in (2, 6):
        weight_term(1, distance)
    feature_term(2)
    feature_send(1)
    scatter_send(1, 2)
    for distance in (1, 7, 0):
        weight_term(1, distance)
    feature_term(0)
    feature_send(2)
    scatter_send(1, 3)
    receive(("df", 0), dr.at[0])
    dk[0] = dk[0] + dr[0].astype(F32)
    scatter_last(1)

    for hh in (0, 1):
        receive(("ow", hh), ow.at[oc, hh])
    for kind, out in ((0, out_k), (1, out_v)):
        for hh in (0, 1):
            for j in range(NY):
                local(
                    ("out", kind, hh, j),
                    ow.at[kind, hh, j],
                    out.at[0, :, pl.ds((2 * j + hh) * HD, HD)],
                ).start()
    for slot in (1, 2, 3):
        receive(("dx", slot), xr.at[slot])
    total = dk[0]
    for slot in (1, 2, 3):
        total = total + xr[slot].astype(F32)
    dx[0] = total.astype(BF)
    local("of", dx.at[0], out_f.at[0]).start()
    for kind, out in ((0, out_k), (1, out_v)):
        for hh in (0, 1):
            for j in range(NY):
                local(
                    ("out", kind, hh, j),
                    ow.at[kind, hh, j],
                    out.at[0, :, pl.ds((2 * j + hh) * HD, HD)],
                ).wait()
    local("of", dx.at[0], out_f.at[0]).wait()
    for copy in started:
        copy.wait_send()
    assert len(ids) <= N_SEMS and len(local_ids) <= 64, (len(ids), len(local_ids))


def per_device(
    queries, grad_out, features, w_key, w_value, q_gain, k_gain, tile_counts, image_starts
):
    hbm = pl.BlockSpec(memory_space=pl.ANY)
    vmem = pl.BlockSpec(memory_space=pltpu.VMEM)
    smem = pl.BlockSpec(memory_space=pltpu.SMEM)
    flops = 3 * 2 * 512 * WIDTH * 2048 + 8 * 8 * 4 * 2 * ROWS * ROWS * HD
    return pl.pallas_call(
        kernel,
        out_shape=(
            jax.ShapeDtypeStruct((1, ROWS, WIDTH), BF),
            jax.ShapeDtypeStruct((1, ROWS, 1024), BF),
            jax.ShapeDtypeStruct((1, ROWS, 1024), BF),
        ),
        in_specs=[hbm, hbm, hbm, hbm, hbm, vmem, vmem, smem, smem],
        out_specs=(hbm, hbm, hbm),
        scratch_shapes=[
            pltpu.VMEM((4, ROWS, WIDTH), BF),
            pltpu.VMEM((4, ROWS, WIDTH), BF),
            pltpu.VMEM((4, 2, ROWS, WIDTH), BF),
            pltpu.VMEM((WIDTH, 8 * ROWS), BF),
            pltpu.VMEM((2, NZ, 2, ROWS, NY * HD), BF),
            pltpu.VMEM((2, 2, NY, 4, ROWS, HD), BF),
            pltpu.VMEM((2, 2, NY, 4, ROWS, HD), BF),
            pltpu.VMEM((2, 2, 4, ROWS, HD), BF),
            pltpu.VMEM((2, NY, 4, 2, ROWS, HD), BF),
            pltpu.VMEM((NZ, 2 * ROWS, NY * HD), F32),
            pltpu.VMEM((2, 2, HALF, 2, ROWS, NY * HD), BF),
            pltpu.VMEM((2, 2, HALF, 2, ROWS, NY * HD), BF),
            pltpu.VMEM((2, NY, ROWS, HD), BF),
            pltpu.VMEM((2, 2, NY, ROWS, HD), BF),
            pltpu.VMEM((4, ROWS, WIDTH), BF),
            pltpu.VMEM((4, ROWS, WIDTH), BF),
            pltpu.VMEM((4, ROWS, WIDTH), F32),
            pltpu.VMEM((4, ROWS, WIDTH), BF),
            pltpu.VMEM((4, ROWS, WIDTH), BF),
            pltpu.SemaphoreType.DMA((N_SEMS,)),
            pltpu.SemaphoreType.DMA((N_SEMS,)),
            pltpu.SemaphoreType.DMA((64,)),
        ],
        compiler_params=pltpu.CompilerParams(
            collective_id=0, has_side_effects=True, vmem_limit_bytes=58 << 20
        ),
        cost_estimate=pl.CostEstimate(
            flops=flops, bytes_accessed=8 << 20, transcendentals=1 << 20
        ),
        name="cross_attention_backward",
    )(queries, grad_out, features, w_key, w_value, q_gain, k_gain, tile_counts, image_starts)


def solution(mesh):
    in_specs = (
        P("pipe", None, "dp", "mp"),
        P("pipe", None, "dp", "mp"),
        P("pipe", "dp", "mp"),
        P("pipe", ("mp", "dp"), None),
        P("pipe", ("mp", "dp"), None),
        P("pipe", None),
        P("pipe", None),
        P(None, "dp", None),
        P(None, "dp", None),
    )
    out_specs = (
        P("pipe", "dp", "mp"),
        P("pipe", ("mp", "dp"), None),
        P("pipe", ("mp", "dp"), None),
    )
    return jax.shard_map(
        per_device, mesh=mesh, in_specs=in_specs, out_specs=out_specs, check_vma=False
    )
```

time: 347 us -> 134 us (0.39)
  waiting for transfers between devices: 249 us -> 0 us
  Pallas kernels: 0 us -> 125 us
  matrix products: 37.6 us -> 0 us
  local copies, waits for them, and re-layouts: 33.8 us -> 7.89 us
  between operations: 14.4 us -> 0.64 us
  other arithmetic: 11.2 us -> 0 us
    all_gather x3 -> x0, waiting for transfers between devices: 140 us -> none  [the longest x1 69 us: per_device(): lax.all_gather(jnp.stack([w_key[0], w_value[0]]), 'dp', axis=1, tiled=True)]
    pallas_call x0 -> x1, Pallas kernels: none -> 125 us  [per_device(): pl.pallas_call(kernel, out_shape=(jax.ShapeDtypeStruct((1, ROWS, WIDTH),...]
    unnamed x7 -> x0, waiting for transfers between devices: 59.7 us -> none
    reduce_scatter x2 -> x0, waiting for transfers between devices: 48.7 us -> none  [the longest x1 34 us: per_device(): lax.psum_scatter(jnp.einsum('bsk,sik->bi', kv_grads, weight_pair, preferr...]
    dot_general x8 -> x0, matrix products: 37.6 us -> none  [the longest x1 10 us: per_device(): jnp.einsum('bi,bsk->isk', flattened, kv_grads, preferred_element_type=jnp...]
    unnamed x30 -> x5, local copies, waits for them, and re-layouts: 27.6 us -> 7.89 us
    convert_element_type x4 -> x0, local copies, waits for them, and re-layouts: 4.92 us -> none  [the longest x1 4.42 us: attention_grads(): score_grad = (probability * (prob_grad - row_delta)).astype(jnp.bfloat16)]
    convert_element_type x3 -> x0, other arithmetic: 4.01 us -> none  [the longest x1 3.81 us: attention_grads(): normed(query.astype(jnp.float32), q_gain).astype(jnp.bfloat16)]
  transfers between devices with their start and end apart: 6 -> 0, of which waited for: 6 -> 0; matrix products, arithmetic and copies ran while one was open for 8% -> 0% of each run, Pallas kernels for 0% -> 0%
where the time goes in v1:
time: 134 us
  Pallas kernels  125 us (93%)
  local copies, waits for them, and re-layouts  7.89 us (6%)
    pallas_call x1, Pallas kernels, per_device(): pl.pallas_call(kernel, out_shape=(jax.ShapeDtypeStruct((1, ROWS, WIDTH),...  125 us
    unnamed x5, local copies, waits for them, and re-layouts  7.89 us

profile of v1, /device:TPU:1, one launch (start us, length us, event | category | flops | bytes accessed | tf_op | source)
XLA Modules:
  0.0 133.9 jit_solution(12303217970023300054)
XLA Ops:
  0.6 1.3 copy.12.tiles
  2.0 1.3 copy.13.starts
  3.3 125.3 %cross_attention_backward.1 = (bf16[1,128,2048]{2,1,0:T(8,128)(2,1)}, bf16[1,128,1024]{2,1,0:T(8,128)(2,1)}, bf16[1,128,1024]{2,1,0:T(8,128)(2,1)}) custom-call(bf16[1,4,128,2048]{3,2,1,0:T(8,128)(2,1)} %queries.1, bf16[1,4,128,2048]{3,2,1,0:T(8,128)(2,1)} %grad_out.1, bf16[1,128,2048]{2,1,0:T(8,128)(2,1)} %features.1, bf16[1,128,1024]{2,1,0:T(8,128)(2,1)} %w_key.1, ...), custom_call_target="tpu_custom_call" | custom-call | flops 13958643712 | bytes 8388608 | tf_op jit(solution)/shard_map/cross_attention_backward/pallas_call | solution.py:571
  128.7 1.9 %copy.17 = bf16[1,128,2048]{2,1,0:T(8,128)(2,1)} copy(bf16[1,128,2048]{2,1,0:T(8,128)(2,1)} %get-tuple-element.6) | data formatting | bytes 1048576
  130.5 1.7 %copy.18 = bf16[1,128,1024]{2,1,0:T(8,128)(2,1)} copy(bf16[1,128,1024]{2,1,0:T(8,128)(2,1)} %get-tuple-element.7) | data formatting | bytes 524288
  132.2 1.7 %copy.19 = bf16[1,128,1024]{2,1,0:T(8,128)(2,1)} copy(bf16[1,128,1024]{2,1,0:T(8,128)(2,1)} %get-tuple-element.8) | data formatting | bytes 524288

commit v2 on v1

--- a/solution.py
+++ b/solution.py
@@ -44,6 +44,7 @@
     wb,
     ps,
     rk,
+    kh,
     gs,
     ga,
     pw,
@@ -53,8 +54,9 @@
     ow,
     ds,
     dr,
-    dk,
+    af,
     dx,
+    xh,
     xr,
     send_sems,
     recv_sems,
@@ -100,6 +102,7 @@
         copy = remote(key, src, dst, device)
         copy.start()
         started.append(copy)
+        return copy
 
     def receive(key, dst):
         remote(key, dst, dst, sibling).wait_recv()
@@ -112,8 +115,8 @@
 
     barrier = pltpu.get_barrier_semaphore()
     partners = [sibling, at_z(1), at_z(NZ - 1)]
-    partners += [at_x(step) for step in (1, 2, 3)]
-    partners += [at_y(step, core) for step in (1, 2, 3) for core in (cc, oc)]
+    partners += [at_x(step) for step in (1, 3)]
+    partners += [at_y(step, core) for step in (1, 3) for core in (cc, oc)]
     for device in partners:
         pl.semaphore_signal(barrier, inc=1, device_id=device, device_id_type=MESH)
 
@@ -161,43 +164,39 @@
     send(("fx", 1), features.at[0], fa.at[1, cc], at_x(3))
     send(("fs", 0), features.at[0], fa.at[0, cc], sibling)
 
-    def gather_pieces(direction, k):
-        if k == HALF - 1:
-            return (direction,)
-        return (0, 1)
-
     def origin(direction, k):
         return (zz - k + NZ) % NZ if direction == RIGHT else (zz + k) % NZ
 
-    def gather_send(hh, k, pieces=(0, 1)):
-        for piece in pieces:
+    def onward(direction):
+        return at_z(1 if direction == RIGHT else NZ - 1)
+
+    in_flight = {}
+
+    def sent(key):
+        for copy in in_flight.pop(key):
+            copy.wait_send()
+            started[:] = [other for other in started if other is not copy]
+
+    def gather(hh, n):
+        k, second = n // 2, n % 2
+        in_flight["ag", hh, n] = copies = []
+        for direction in (RIGHT, LEFT):
+            piece = 1 - direction if second else direction
+            block = wb.at[hh, origin(direction, k), piece]
+            if k:
+                receive(("ag", direction, hh, k - 1, piece), block)
+            copies.append(
+                send(("ag", direction, hh, k, piece), block, block, onward(direction))
+            )
+
+    def gather_done(hh):
+        for k, second in ((HALF - 2, 1), (HALF - 1, 0)):
             for direction in (RIGHT, LEFT):
-                if piece not in gather_pieces(direction, k):
-                    continue
-                block = wb.at[hh, origin(direction, k), piece]
-                if k:
-                    receive(("ag", direction, hh, k - 1, piece), block)
-                send(
+                piece = 1 - direction if second else direction
+                receive(
                     ("ag", direction, hh, k, piece),
-                    block,
-                    block,
-                    at_z(1 if direction == RIGHT else NZ - 1),
-                )
-
-    def gather_rest(hh):
-        for direction in (RIGHT, LEFT):
-            piece = 1 - direction
-            receive(
-                ("ag", direction, hh, HALF - 2, piece),
-                wb.at[hh, origin(direction, HALF - 1), piece],
-            )
-
-    def gather_last(hh):
-        for direction in (RIGHT, LEFT):
-            receive(
-                ("ag", direction, hh, HALF - 1, direction),
-                wb.at[hh, origin(direction, HALF), direction],
-            )
+                    wb.at[hh, origin(direction, k + 1), piece],
+                )
 
     def own_weights(hh):
         for j in range(NY):
@@ -250,27 +249,53 @@
             return carry
 
         lax.fori_loop(0, 2, body, 0)
+        far = (qy + 2) % NY
+        for way, slot in ((RIGHT, 2 * mg), (LEFT, 2 * mg + 1)):
+            send(
+                ("kh", hh, mg, way),
+                ps.at[hh, :, far, slot],
+                kh.at[hh, mg, way],
+                at_y(1 if way == RIGHT else 3, cc),
+            )
+        for way, slot in ((RIGHT, 2 * mg + 1), (LEFT, 2 * mg)):
+            send_keys(hh, way, slot)
         pair = pl.ds(2 * mg, 2)
-        for step in (2, 1, 3, 0):
-            target = (qy + step) % NY
-            for same in (1, 0):
-                core = cc if same else oc
-                src = ps.at[hh, core, target, pair]
-                dst = rk.at[hh, cc, step, pair]
-                if step == 0 and same:
-                    local(("kv", hh, mg), src, dst).start()
-                else:
-                    send(("kv", hh, mg, step, same), src, dst, at_y(step, core))
+        send(("kv", hh, mg), ps.at[hh, oc, qy, pair], rk.at[hh, cc, 0, pair], sibling)
+        local(("kv", hh, mg), ps.at[hh, cc, qy, pair], rk.at[hh, cc, 0, pair]).start()
+
+    def send_keys(hh, way, slot):
+        step = 1 if way == RIGHT else 3
+        for same in (1, 0):
+            core = cc if same else oc
+            send(
+                ("ky", hh, way, slot, same),
+                ps.at[hh, core, (qy + step) % NY, slot],
+                rk.at[hh, cc, 1 + way, slot],
+                at_y(step, core),
+            )
+
+    def relay_keys(hh, mg):
+        for way, slot in ((RIGHT, 2 * mg), (LEFT, 2 * mg + 1)):
+            target = (qy + (1 if way == RIGHT else 3)) % NY
+            receive(("kh", hh, mg, way), kh.at[hh, mg, way])
+            for replica in (0, 1):
+                ps[hh, replica, target, slot] = (
+                    ps[hh, replica, target, slot].astype(F32)
+                    + kh[hh, mg, way, replica].astype(F32)
+                ).astype(BF)
+            send_keys(hh, way, slot)
 
     def projected(hh, mg):
         pair = pl.ds(2 * mg, 2)
-        for step in range(NY):
-            for same in (1, 0):
-                dst = rk.at[hh, cc if same else oc, step, pair]
-                if step == 0 and same:
-                    local(("kv", hh, mg), dst, dst).wait()
-                else:
-                    receive(("kv", hh, mg, step, same), dst)
+        local(("kv", hh, mg), rk.at[hh, cc, 0, pair], rk.at[hh, cc, 0, pair]).wait()
+        receive(("kv", hh, mg), rk.at[hh, oc, 0, pair])
+        for way in (RIGHT, LEFT):
+            for slot in (2 * mg, 2 * mg + 1):
+                for same in (1, 0):
+                    receive(
+                        ("ky", hh, way, slot, same),
+                        rk.at[hh, cc if same else oc, 1 + way, slot],
+                    )
 
     root_scale = 1.0 / math.sqrt(HD)
 
@@ -282,7 +307,7 @@
             micro = (px + i) % NX if mg == 0 else (px + 3 - i) % NX
             key_pre = rk[hh, 0, 0, slot].astype(F32)
             value = rk[hh, 1, 0, slot].astype(F32)
-            for step in range(1, NY):
+            for step in (1, 2):
                 key_pre += rk[hh, 0, step, slot].astype(F32)
                 value += rk[hh, 1, step, slot].astype(F32)
             value = value.astype(BF)
@@ -292,10 +317,10 @@
             key = (key_pre * inverse * gain).astype(BF)
             slots = lax.broadcasted_iota(jnp.int32, (ROWS, 2 * ROWS), 0)
             texts = lax.broadcasted_iota(jnp.int32, (ROWS, 2 * ROWS), 1) % ROWS
-            first = tiles[micro, 0, 0] * TILE_TOK
-            second = first + tiles[micro, 0, 1] * TILE_TOK
-            seen = ((slots < first) & (texts >= starts[micro, 0, 0])) | (
-                (slots >= first) & (slots < second) & (texts >= starts[micro, 0, 1])
+            first = tiles[0, 0, micro] * TILE_TOK
+            second = first + tiles[0, 1, micro] * TILE_TOK
+            seen = ((slots < first) & (texts >= starts[0, 0, micro])) | (
+                (slots >= first) & (slots < second) & (texts >= starts[0, 1, micro])
             )
             visible = jnp.where(seen, 1.0, 0.0).astype(F32)
             value_grad = jnp.zeros((ROWS, HD), F32)
@@ -331,7 +356,7 @@
 
         lax.fori_loop(0, 2, body, 0)
         pair = pl.ds(2 * mg, 2)
-        for step in (2, 1, 3, 0):
+        for step in (1, 3, 0):
             for same in (1, 0):
                 kind = cc if same else oc
                 src = gs.at[hh, kind, pair]
@@ -341,16 +366,24 @@
                 else:
                     send(("g", hh, mg, step, same), src, dst, at_y(step, kind))
 
+    def relay_grads(hh, mg):
+        for step, slot in ((1, 2 * mg), (3, 2 * mg + 1)):
+            source = (qy - step + NY) % NY
+            for same in (1, 0):
+                receive(
+                    ("g", hh, mg, step, same),
+                    ga.at[hh, source, pl.ds(2 * mg, 2), cc if same else oc],
+                )
+            block = ga.at[hh, source, slot]
+            send(("gh", hh, mg, step), block, block, at_y(step, cc))
+
     def gathered(hh, mg):
         pair = pl.ds(2 * mg, 2)
-        for step in range(NY):
-            source = (qy - step + NY) % NY
-            for same in (1, 0):
-                dst = ga.at[hh, source, pair, cc if same else oc]
-                if step == 0 and same:
-                    local(("g", hh, mg), dst, dst).wait()
-                else:
-                    receive(("g", hh, mg, step, same), dst)
+        dst = ga.at[hh, qy, pair, cc]
+        local(("g", hh, mg), dst, dst).wait()
+        receive(("g", hh, mg, 0, 0), ga.at[hh, qy, pair, oc])
+        for step, slot in ((1, 2 * mg), (3, 2 * mg + 1)):
+            receive(("gh", hh, mg, step), ga.at[hh, (qy + 2) % NY, slot])
 
     def weight_term(hh, distance):
         block = (zz + distance) % NZ
@@ -361,36 +394,35 @@
             grads = jnp.concatenate(
                 [ga[hh, n * 2 + j].reshape(8 * ROWS, HD) for j in (0, 1)], axis=1
             )
-            pw[distance, :, columns] = jnp.dot(lhs, grads, preferred_element_type=F32)
+            pw[hh, distance, :, columns] = jnp.dot(lhs, grads, preferred_element_type=F32)
             return carry
 
         lax.fori_loop(0, 2, body, 0)
 
-    def scatter_pieces(direction, k):
-        return (direction,) if k == 0 else (0, 1)
-
-    def scatter_send(hh, k, pieces=(0, 1)):
-        for piece in pieces:
-            for direction in (RIGHT, LEFT):
-                if piece not in scatter_pieces(direction, k):
-                    continue
-                distance = HALF - k if direction == RIGHT else HALF + k
-                total = pw[distance, piece * ROWS : (piece + 1) * ROWS, :]
-                if k and piece in scatter_pieces(direction, k - 1):
-                    arrived = rb.at[hh, direction, k - 1, piece]
-                    receive(("rs", direction, hh, k - 1, piece), arrived)
-                    total = total + arrived[...].astype(F32)
-                sb[hh, direction, k, piece] = total.astype(BF)
+    def scatter(hh, n):
+        k, second = (n + 1) // 2, n % 2
+        in_flight["rs", hh, n] = copies = []
+        for direction in (RIGHT, LEFT):
+            piece = 1 - direction if second else direction
+            distance = HALF - k if direction == RIGHT else HALF + k
+            total = pw[hh, distance, piece * ROWS : (piece + 1) * ROWS, :]
+            if n > 1:
+                arrived = rb.at[hh, direction, k - 1, piece]
+                receive(("rs", direction, hh, k - 1, piece), arrived)
+                total = total + arrived[...].astype(F32)
+            sb[hh, direction, k, piece] = total.astype(BF)
+            copies.append(
                 send(
                     ("rs", direction, hh, k, piece),
                     sb.at[hh, direction, k, piece],
                     rb.at[hh, direction, k, piece],
-                    at_z(1 if direction == RIGHT else NZ - 1),
-                )
+                    onward(direction),
+                )
+            )
 
     factor = 1.0 / (NX * NZ * 2)
 
-    def scatter_last(hh):
+    def scatter_done(hh):
         for direction in (RIGHT, LEFT):
             for piece in (0, 1):
                 receive(
@@ -399,7 +431,7 @@
 
         def finished(piece):
             total = (
-                pw[0, pl.ds(pl.multiple_of(piece * ROWS, ROWS), ROWS), :]
+                pw[hh, 0, pl.ds(pl.multiple_of(piece * ROWS, ROWS), ROWS), :]
                 + rb[hh, RIGHT, HALF - 1, piece].astype(F32)
                 + rb[hh, LEFT, HALF - 1, piece].astype(F32)
             )
@@ -413,122 +445,177 @@
         for j in range(NY):
             ow[cc, hh, j] = own[:, j * HD : (j + 1) * HD]
 
-    def feature_term(slot):
+    def feature_term(hh, pair):
         def body(n, carry):
             columns = pl.ds(pl.multiple_of(n * 256, 256), 256)
-            total = jnp.zeros((2 * ROWS, 256), F32)
-            for hh in (0, 1):
-                grads = jnp.concatenate(
-                    [ga[hh, j, slot].reshape(2 * ROWS, HD) for j in range(NY)], axis=1
-                )
-                weights = wb[hh, n].reshape(256, NY * HD)
-                total += lax.dot_general(grads, weights, NT, preferred_element_type=F32)
-            pieces = (total[:ROWS], total[ROWS:])
-            mine = jnp.where(cc == 0, pieces[0], pieces[1])
-            others = jnp.where(cc == 0, pieces[1], pieces[0])
-            dk[slot, :, columns] = mine
-            ds[slot, :, columns] = others.astype(BF)
+            grads = jnp.concatenate(
+                [ga[hh, j, 2 * pair : 2 * pair + 2].reshape(4 * ROWS, HD) for j in range(NY)],
+                axis=1,
+            )
+            weights = wb[hh, n].reshape(256, NY * HD)
+            total = lax.dot_general(grads, weights, NT, preferred_element_type=F32)
+            for i in (0, 1):
+                slot = 2 * pair + i
+                terms = [total[(2 * i + r) * ROWS : (2 * i + r + 1) * ROWS] for r in (0, 1)]
+                if hh == 0:
+                    for r in (0, 1):
+                        af[slot, r, :, columns] = terms[r]
+                else:
+                    terms = [terms[r] + af[slot, r, :, columns] for r in (0, 1)]
+                    af[slot, 0, :, columns] = jnp.where(cc == 0, terms[0], terms[1])
+                    ds[slot, :, columns] = jnp.where(cc == 0, terms[1], terms[0]).astype(BF)
             return carry
 
         lax.fori_loop(0, NZ, body, 0)
-        send(("df", slot), ds.at[slot], dr.at[slot], sibling)
-
-    def feature_send(slot):
-        receive(("df", slot), dr.at[slot])
-        dx[slot] = (dk[slot] + dr[slot].astype(F32)).astype(BF)
-        send(("dx", slot), dx.at[slot], xr.at[slot], at_x(OFFSETS[slot]))
+        if hh == 1:
+            for slot in (2 * pair + 1, 2 * pair):
+                send(("df", slot), ds.at[slot], dr.at[slot], sibling)
+
+    half = ROWS // 2
+
+    def feature_far():
+        receive(("df", 3), dr.at[3])
+        dx[3] = (af[3, 0] + dr[3].astype(F32)).astype(BF)
+        for way in (RIGHT, LEFT):
+            send(
+                ("xh", way),
+                dx.at[3, pl.ds(way * half, half)],
+                xh.at[way],
+                at_x(1 if way == RIGHT else 3),
+            )
+
+    def feature_send(way, second):
+        slot = 1 if way == RIGHT else 2
+        low = half * (way if second else 1 - way)
+        total = af[slot, 0, low : low + half] + dr[slot, low : low + half].astype(F32)
+        if second:
+            receive(("xh", way), xh.at[way])
+            total = total + xh[way].astype(F32)
+        dx[slot, low : low + half] = total.astype(BF)
+        rows = pl.ds(low, half)
+        send(
+            ("xr", way, second),
+            dx.at[slot, rows],
+            xr.at[way, rows],
+            at_x(1 if way == RIGHT else 3),
+        )
 
     own_weights(0)
-    gather_send(0, 0)
-    for slot in range(NX):
-        norm_queries(slot)
+    gather(0, 0)
+    norm_queries(0)
+    sent(("ag", 0, 0))
+    gather(0, 1)
+    norm_queries(1)
+    gather(0, 2)
+    norm_queries(2)
+    gather(0, 3)
+    norm_queries(3)
     local("f", fa.at[0, cc], fa.at[0, cc]).wait()
     transpose_features(0, cc)
-    gather_send(0, 1, (0,))
+    gather(0, 4)
     receive(("fs", 0), fa.at[0, oc])
     transpose_features(0, oc)
-    gather_send(0, 1, (1,))
-    gather_send(0, 2, (0,))
+    gather(0, 5)
     receive(("fx", 1), fa.at[1, cc])
     send(("fh", 0), fa.at[1, cc, pl.ds(0, 64)], fa.at[3, cc, pl.ds(0, 64)], at_x(3))
     receive(("fx", 3), fa.at[2, cc])
     send(("fh", 1), fa.at[2, cc, pl.ds(64, 64)], fa.at[3, cc, pl.ds(64, 64)], at_x(1))
     send(("fs", 1), fa.at[1, cc], fa.at[1, cc], sibling)
     send(("fs", 2), fa.at[2, cc], fa.at[2, cc], sibling)
-    gather_send(0, 2, (1,))
+    own_weights(1)
+    gather(0, 6)
     transpose_features(1, cc)
     transpose_features(2, cc)
-    gather_send(0, 3)
-    gather_rest(0)
-    own_weights(1)
-    gather_send(1, 0)
+    sent(("ag", 0, 5))
+    gather(1, 0)
     receive(("fh", 0), fa.at[3, cc, pl.ds(0, 64)])
     receive(("fh", 1), fa.at[3, cc, pl.ds(64, 64)])
     send(("fs", 3), fa.at[3, cc], fa.at[3, cc], sibling)
-    gather_last(0)
+    sent(("ag", 0, 6))
+    gather(1, 1)
+    gather_done(0)
     receive(("fs", 1), fa.at[1, oc])
     project(0, 0)
-    gather_send(1, 1, (0,))
+    gather(1, 2)
     receive(("fs", 2), fa.at[2, oc])
     receive(("fs", 3), fa.at[3, oc])
     project(0, 1)
-    gather_send(1, 1, (1,))
+    gather(1, 3)
     transpose_features(1, oc)
+    relay_keys(0, 0)
     transpose_features(2, oc)
+    relay_keys(0, 1)
+    gather(1, 4)
     transpose_features(3, cc)
     transpose_features(3, oc)
     for slot in range(NX):
         local(("d", slot), do.at[slot], do.at[slot]).wait()
-    gather_send(1, 2, (0,))
     projected(0, 0)
     attend(0, 0)
-    gather_send(1, 2, (1,))
+    gather(1, 5)
     projected(0, 1)
     attend(0, 1)
-    gather_send(1, 3)
-    gather_rest(1)
-    gather_last(1)
+    gather(1, 6)
+    relay_grads(0, 0)
+    relay_grads(0, 1)
+    gather_done(1)
     project(1, 0)
     project(1, 1)
     gathered(0, 0)
     gathered(0, 1)
-    weight_term(0, HALF)
-    scatter_send(0, 0)
-    for distance in (3, 5, 2, 6):
-        weight_term(0, distance)
-    scatter_send(0, 1)
+    weight_term(0, 4)
+    scatter(0, 0)
+    weight_term(0, 3)
+    weight_term(0, 5)
+    sent(("rs", 0, 0))
+    scatter(0, 1)
+    relay_keys(1, 0)
+    relay_keys(1, 1)
+    weight_term(0, 2)
+    weight_term(0, 6)
+    scatter(0, 2)
     for distance in (1, 7, 0):
         weight_term(0, distance)
+    scatter(0, 3)
     projected(1, 0)
     attend(1, 0)
-    scatter_send(0, 2)
+    scatter(0, 4)
     projected(1, 1)
     attend(1, 1)
-    scatter_send(0, 3)
-    scatter_last(0)
+    scatter(0, 5)
+    relay_grads(1, 0)
+    feature_term(0, 1)
+    scatter(0, 6)
+    relay_grads(1, 1)
+    feature_term(0, 0)
     gathered(1, 0)
     gathered(1, 1)
-    weight_term(1, HALF)
-    scatter_send(1, 0)
-    for distance in (3, 5):
-        weight_term(1, distance)
-    feature_term(3)
-    scatter_send(1, 1)
-    feature_term(1)
-    feature_send(3)
+    weight_term(1, 4)
+    scatter(1, 0)
+    weight_term(1, 3)
+    weight_term(1, 5)
+    scatter(1, 1)
+    feature_term(1, 1)
+    scatter(1, 2)
     for distance in (2, 6):
         weight_term(1, distance)
-    feature_term(2)
-    feature_send(1)
-    scatter_send(1, 2)
+    feature_far()
+    scatter(1, 3)
+    receive(("df", 2), dr.at[2])
+    feature_send(LEFT, 0)
+    feature_term(1, 0)
+    scatter(1, 4)
+    receive(("df", 1), dr.at[1])
+    feature_send(RIGHT, 0)
     for distance in (1, 7, 0):
         weight_term(1, distance)
-    feature_term(0)
-    feature_send(2)
-    scatter_send(1, 3)
+    scatter(1, 5)
+    feature_send(LEFT, 1)
+    feature_send(RIGHT, 1)
+    scatter_done(0)
     receive(("df", 0), dr.at[0])
-    dk[0] = dk[0] + dr[0].astype(F32)
-    scatter_last(1)
+    scatter(1, 6)
+    scatter_done(1)
 
     for hh in (0, 1):
         receive(("ow", hh), ow.at[oc, hh])
@@ -540,11 +627,13 @@
                     ow.at[kind, hh, j],
                     out.at[0, :, pl.ds((2 * j + hh) * HD, HD)],
                 ).start()
-    for slot in (1, 2, 3):
-        receive(("dx", slot), xr.at[slot])
-    total = dk[0]
-    for slot in (1, 2, 3):
-        total = total + xr[slot].astype(F32)
+    for way in (RIGHT, LEFT):
+        for second in (0, 1):
+            low = half * (way if second else 1 - way)
+            receive(("xr", way, second), xr.at[way, pl.ds(low, half)])
+    total = af[0, 0] + dr[0].astype(F32)
+    for way in (RIGHT, LEFT):
+        total = total + xr[way].astype(F32)
     dx[0] = total.astype(BF)
     local("of", dx.at[0], out_f.at[0]).start()
     for kind, out in ((0, out_k), (1, out_v)):
@@ -561,14 +650,29 @@
     assert len(ids) <= N_SEMS and len(local_ids) <= 64, (len(ids), len(local_ids))
 
 
+def copy_results(a, b, c, x, y, z, hold_a, hold_b, hold_c, sems):
+    parts = ((a, hold_a, x), (b, hold_b, y), (c, hold_c, z))
+    reads = [pltpu.make_async_copy(p[0], p[1], sems.at[n]) for n, p in enumerate(parts)]
+    writes = [pltpu.make_async_copy(p[1], p[2], sems.at[3 + n]) for n, p in enumerate(parts)]
+    for copy in reads:
+        copy.start()
+    for n in range(3):
+        reads[n].wait()
+        writes[n].start()
+    for copy in writes:
+        copy.wait()
+
+
 def per_device(
     queries, grad_out, features, w_key, w_value, q_gain, k_gain, tile_counts, image_starts
 ):
     hbm = pl.BlockSpec(memory_space=pl.ANY)
     vmem = pl.BlockSpec(memory_space=pltpu.VMEM)
     smem = pl.BlockSpec(memory_space=pltpu.SMEM)
+    tiles = jnp.transpose(tile_counts, (1, 2, 0))
+    starts = jnp.transpose(image_starts, (1, 2, 0))
     flops = 3 * 2 * 512 * WIDTH * 2048 + 8 * 8 * 4 * 2 * ROWS * ROWS * HD
-    return pl.pallas_call(
+    results = pl.pallas_call(
         kernel,
         out_shape=(
             jax.ShapeDtypeStruct((1, ROWS, WIDTH), BF),
@@ -584,19 +688,21 @@
             pltpu.VMEM((WIDTH, 8 * ROWS), BF),
             pltpu.VMEM((2, NZ, 2, ROWS, NY * HD), BF),
             pltpu.VMEM((2, 2, NY, 4, ROWS, HD), BF),
-            pltpu.VMEM((2, 2, NY, 4, ROWS, HD), BF),
+            pltpu.VMEM((2, 2, 3, 4, ROWS, HD), BF),
+            pltpu.VMEM((2, 2, 2, 2, ROWS, HD), BF),
             pltpu.VMEM((2, 2, 4, ROWS, HD), BF),
             pltpu.VMEM((2, NY, 4, 2, ROWS, HD), BF),
-            pltpu.VMEM((NZ, 2 * ROWS, NY * HD), F32),
+            pltpu.VMEM((2, NZ, 2 * ROWS, NY * HD), F32),
             pltpu.VMEM((2, 2, HALF, 2, ROWS, NY * HD), BF),
             pltpu.VMEM((2, 2, HALF, 2, ROWS, NY * HD), BF),
             pltpu.VMEM((2, NY, ROWS, HD), BF),
             pltpu.VMEM((2, 2, NY, ROWS, HD), BF),
             pltpu.VMEM((4, ROWS, WIDTH), BF),
             pltpu.VMEM((4, ROWS, WIDTH), BF),
-            pltpu.VMEM((4, ROWS, WIDTH), F32),
+            pltpu.VMEM((4, 2, ROWS, WIDTH), F32),
             pltpu.VMEM((4, ROWS, WIDTH), BF),
-            pltpu.VMEM((4, ROWS, WIDTH), BF),
+            pltpu.VMEM((2, 64, WIDTH), BF),
+            pltpu.VMEM((2, ROWS, WIDTH), BF),
             pltpu.SemaphoreType.DMA((N_SEMS,)),
             pltpu.SemaphoreType.DMA((N_SEMS,)),
             pltpu.SemaphoreType.DMA((64,)),
@@ -608,7 +714,16 @@
             flops=flops, bytes_accessed=8 << 20, transcendentals=1 << 20
         ),
         name="cross_attention_backward",
-    )(queries, grad_out, features, w_key, w_value, q_gain, k_gain, tile_counts, image_starts)
+    )(queries, grad_out, features, w_key, w_value, q_gain, k_gain, tiles, starts)
+    return pl.pallas_call(
+        copy_results,
+        out_shape=tuple(jax.ShapeDtypeStruct(r.shape, r.dtype) for r in results),
+        in_specs=[hbm, hbm, hbm],
+        out_specs=(hbm, hbm, hbm),
+        scratch_shapes=[pltpu.VMEM(r.shape, r.dtype) for r in results]
+        + [pltpu.SemaphoreType.DMA((6,))],
+        name="copy_results",
+    )(*results)
 
 
 def solution(mesh):

time: 134 us -> 119 us (0.89)
  local copies, waits for them, and re-layouts: 7.89 us -> 0 us
  Pallas kernels: 125 us -> 118 us
    pallas_call x1, Pallas kernels: 125 us -> 116 us  [per_device(): pl.pallas_call(kernel, out_shape=(jax.ShapeDtypeStruct((1, ROWS, WIDTH),...]
    unnamed x5 -> x0, local copies, waits for them, and re-layouts: 7.89 us -> none
    pallas_call x0 -> x1, Pallas kernels: none -> 2.06 us  [per_device(): pl.pallas_call(copy_results, out_shape=tuple((jax.ShapeDtypeStruct(r.shap...]
where the time goes in v2:
time: 119 us
  Pallas kernels  118 us (99%)
    pallas_call x1, Pallas kernels, per_device(): pl.pallas_call(kernel, out_shape=(jax.ShapeDtypeStruct((1, ROWS, WIDTH),...  116 us

profile of v2, /device:TPU:1, one launch (start us, length us, event | category | flops | bytes accessed | tf_op | source)
XLA Modules:
  0.0 119.0 jit_solution(12468557070847107896)
XLA Ops:
  0.6 116.2 %cross_attention_backward.1 = (bf16[1,128,2048]{2,1,0:T(8,128)(2,1)}, bf16[1,128,1024]{2,1,0:T(8,128)(2,1)}, bf16[1,128,1024]{2,1,0:T(8,128)(2,1)}) custom-call(bf16[1,4,128,2048]{3,2,1,0:T(8,128)(2,1)} %queries.1, bf16[1,4,128,2048]{3,2,1,0:T(8,128)(2,1)} %grad_out.1, bf16[1,128,2048]{2,1,0:T(8,128)(2,1)} %features.1, bf16[1,128,1024]{2,1,0:T(8,128)(2,1)} %w_key.1, ...), custom_call_target="tpu_custom_call" | custom-call | flops 13958643712 | bytes 8388608 | tf_op jit(solution)/shard_map/cross_attention_backward/pallas_call | solution.py:675
  116.8 2.1 %copy_results.1 = (bf16[1,128,2048]{2,1,0:T(8,128)(2,1)}, bf16[1,128,1024]{2,1,0:T(8,128)(2,1)}, bf16[1,128,1024]{2,1,0:T(8,128)(2,1)}) custom-call(bf16[1,128,2048]{2,1,0:T(8,128)(2,1)} %get-tuple-element.6.a, bf16[1,128,1024]{2,1,0:T(8,128)(2,1)} %get-tuple-element.7.b, bf16[1,128,1024]{2,1,0:T(8,128)(2,1)} %get-tuple-element.8.c), custom_call_target="tpu_custom_call" | custom-call | tf_op jit(solution)/shard_map/copy_results/pallas_call | solution.py:718

commit v3 on v2

--- a/solution.py
+++ b/solution.py
@@ -104,14 +104,23 @@
         started.append(copy)
         return copy
 
+    waited = set()
+
     def receive(key, dst):
-        remote(key, dst, dst, sibling).wait_recv()
+        if key not in waited:
+            waited.add(key)
+            remote(key, dst, dst, sibling).wait_recv()
 
     local_ids = {}
 
     def local(key, src, dst):
         n = local_ids.setdefault(key, len(local_ids))
         return pltpu.make_async_copy(src, dst, local_sems.at[n])
+
+    def loaded(key, dst):
+        if key not in waited:
+            waited.add(key)
+            local(key, dst, dst).wait()
 
     barrier = pltpu.get_barrier_semaphore()
     partners = [sibling, at_z(1), at_z(NZ - 1)]
@@ -130,7 +139,7 @@
             for hh in (0, 1):
                 for j in range(NY):
                     local(
-                        ("w", hh, j),
+                        ("lw", hh, j),
                         weight_columns(kinds[kind], hh, j),
                         wb.at[hh, zz, cc, :, pl.ds(j * HD, HD)],
                     ).start()
@@ -179,6 +188,11 @@
 
     def gather(hh, n):
         k, second = n // 2, n % 2
+        if n == 0:
+            own_weights(hh)
+        before = {(0, 1): (0, 0), (1, 0): (0, 5), (1, 1): (0, 6)}.get((hh, n))
+        if before:
+            sent(("ag", *before))
         in_flight["ag", hh, n] = copies = []
         for direction in (RIGHT, LEFT):
             piece = 1 - direction if second else direction
@@ -201,13 +215,13 @@
     def own_weights(hh):
         for j in range(NY):
             piece = wb.at[hh, zz, cc, :, pl.ds(j * HD, HD)]
-            local(("w", hh, j), piece, piece).wait()
+            loaded(("lw", hh, j), piece)
         for j in range(NY):
             piece = wb.at[hh, zz, oc, :, pl.ds(j * HD, HD)]
             receive(("w", hh, j), piece)
 
     def norm_queries(slot):
-        local(("q", slot), qb.at[slot], qb.at[slot]).wait()
+        loaded(("q", slot), qb.at[slot])
         gain = q_gain[...]
 
         def body(i, carry):
@@ -222,7 +236,31 @@
 
         lax.fori_loop(0, WIDTH // HD // 4, body, 0)
 
-    def transpose_features(slot, replica):
+    def features_ready(slot, same):
+        block = fa.at[slot, cc if same else oc]
+        if not same:
+            receive(("fs", slot), block)
+        elif slot == 0:
+            loaded("f", block)
+        elif slot == 3:
+            for way in (0, 1):
+                receive(("fh", way), fa.at[3, cc, pl.ds(way * 64, 64)])
+        else:
+            receive(("fx", 1 if slot == 1 else 3), block)
+
+    def relay_features(way):
+        slot, rows = 1 + way, pl.ds(way * 64, 64)
+        features_ready(slot, 1)
+        send(("fh", way), fa.at[slot, cc, rows], fa.at[3, cc, rows], at_x(3 if way == 0 else 1))
+        send(("fs", slot), fa.at[slot, cc], fa.at[slot, cc], sibling)
+
+    def far_features():
+        features_ready(3, 1)
+        send(("fs", 3), fa.at[3, cc], fa.at[3, cc], sibling)
+
+    def transpose_features(slot, same):
+        features_ready(slot, same)
+        replica = cc if same else oc
         place = pl.multiple_of((slot * 2 + replica) * ROWS, ROWS)
 
         def body(i, carry):
@@ -234,6 +272,11 @@
         lax.fori_loop(0, WIDTH // HD // 2, body, 0)
 
     def project(hh, mg):
+        gather_done(hh)
+        for slot in (2 * mg, 2 * mg + 1):
+            for same in (1, 0):
+                features_ready(slot, same)
+
         def body(n, carry):
             rows = fa[2 * mg : 2 * mg + 2].reshape(4 * ROWS, WIDTH)
             columns = pl.ds(pl.multiple_of(n * 256, 256), 256)
@@ -257,11 +300,12 @@
                 kh.at[hh, mg, way],
                 at_y(1 if way == RIGHT else 3, cc),
             )
-        for way, slot in ((RIGHT, 2 * mg + 1), (LEFT, 2 * mg)):
-            send_keys(hh, way, slot)
-        pair = pl.ds(2 * mg, 2)
-        send(("kv", hh, mg), ps.at[hh, oc, qy, pair], rk.at[hh, cc, 0, pair], sibling)
-        local(("kv", hh, mg), ps.at[hh, cc, qy, pair], rk.at[hh, cc, 0, pair]).start()
+        for slot in (2 * mg, 2 * mg + 1):
+            send(("kv", hh, slot), ps.at[hh, oc, qy, slot], rk.at[hh, cc, 0, slot], sibling)
+            local(("lk", hh, slot), ps.at[hh, cc, qy, slot], rk.at[hh, cc, 0, slot]).start()
+
+    def near_keys(hh, mg, way):
+        send_keys(hh, way, 2 * mg + 1 - way)
 
     def send_keys(hh, way, slot):
         step = 1 if way == RIGHT else 3
@@ -274,118 +318,112 @@
                 at_y(step, core),
             )
 
-    def relay_keys(hh, mg):
-        for way, slot in ((RIGHT, 2 * mg), (LEFT, 2 * mg + 1)):
-            target = (qy + (1 if way == RIGHT else 3)) % NY
-            receive(("kh", hh, mg, way), kh.at[hh, mg, way])
-            for replica in (0, 1):
-                ps[hh, replica, target, slot] = (
-                    ps[hh, replica, target, slot].astype(F32)
-                    + kh[hh, mg, way, replica].astype(F32)
-                ).astype(BF)
-            send_keys(hh, way, slot)
-
-    def projected(hh, mg):
-        pair = pl.ds(2 * mg, 2)
-        local(("kv", hh, mg), rk.at[hh, cc, 0, pair], rk.at[hh, cc, 0, pair]).wait()
-        receive(("kv", hh, mg), rk.at[hh, oc, 0, pair])
+    def relay_keys(hh, mg, way):
+        slot = 2 * mg + way
+        target = (qy + (1 if way == RIGHT else 3)) % NY
+        receive(("kh", hh, mg, way), kh.at[hh, mg, way])
+        for replica in (0, 1):
+            ps[hh, replica, target, slot] = (
+                ps[hh, replica, target, slot].astype(F32) + kh[hh, mg, way, replica].astype(F32)
+            ).astype(BF)
+        send_keys(hh, way, slot)
+
+    def projected(hh, slot):
+        loaded(("lk", hh, slot), rk.at[hh, cc, 0, slot])
+        receive(("kv", hh, slot), rk.at[hh, oc, 0, slot])
         for way in (RIGHT, LEFT):
-            for slot in (2 * mg, 2 * mg + 1):
-                for same in (1, 0):
-                    receive(
-                        ("ky", hh, way, slot, same),
-                        rk.at[hh, cc if same else oc, 1 + way, slot],
-                    )
+            for same in (1, 0):
+                receive(
+                    ("ky", hh, way, slot, same), rk.at[hh, cc if same else oc, 1 + way, slot]
+                )
 
     root_scale = 1.0 / math.sqrt(HD)
 
-    def attend(hh, mg):
+    def attend(hh, slot):
+        projected(hh, slot)
+        loaded(("d", slot), do.at[slot])
         gain = k_gain[...]
-
-        def body(i, carry):
-            slot = 2 * mg + i
-            micro = (px + i) % NX if mg == 0 else (px + 3 - i) % NX
-            key_pre = rk[hh, 0, 0, slot].astype(F32)
-            value = rk[hh, 1, 0, slot].astype(F32)
-            for step in (1, 2):
-                key_pre += rk[hh, 0, step, slot].astype(F32)
-                value += rk[hh, 1, step, slot].astype(F32)
-            value = value.astype(BF)
-            inverse = lax.rsqrt(
-                jnp.mean(key_pre * key_pre, axis=-1, keepdims=True) + EPSILON
-            )
-            key = (key_pre * inverse * gain).astype(BF)
-            slots = lax.broadcasted_iota(jnp.int32, (ROWS, 2 * ROWS), 0)
-            texts = lax.broadcasted_iota(jnp.int32, (ROWS, 2 * ROWS), 1) % ROWS
-            first = tiles[0, 0, micro] * TILE_TOK
-            second = first + tiles[0, 1, micro] * TILE_TOK
-            seen = ((slots < first) & (texts >= starts[0, 0, micro])) | (
-                (slots >= first) & (slots < second) & (texts >= starts[0, 1, micro])
-            )
-            visible = jnp.where(seen, 1.0, 0.0).astype(F32)
-            value_grad = jnp.zeros((ROWS, HD), F32)
-            normed_grad = jnp.zeros((ROWS, HD), F32)
-            for g in range(0, GROUPS, 2):
-                low = (hh * GROUPS + g) * HD
-                query = jnp.concatenate(
-                    [qb[slot, :, low : low + HD], qb[slot, :, low + HD : low + 2 * HD]], axis=0
-                )
-                grad = jnp.concatenate(
-                    [do[slot, :, low : low + HD], do[slot, :, low + HD : low + 2 * HD]], axis=0
-                )
-                scores = (
-                    lax.dot_general(key, query, NT, preferred_element_type=F32) * root_scale
-                )
-                weights = jnp.exp(scores) * visible
-                total = jnp.sum(weights, axis=0, keepdims=True)
-                probability = weights * (1.0 / jnp.where(total > 0, total, 1.0))
-                prob_grad = lax.dot_general(value, grad, NT, preferred_element_type=F32)
-                delta = jnp.sum(probability * prob_grad, axis=0, keepdims=True)
-                score_grad = (probability * (prob_grad - delta)).astype(BF)
-                value_grad += jnp.dot(
-                    probability.astype(BF), grad, preferred_element_type=F32
-                )
-                normed_grad += jnp.dot(score_grad, query, preferred_element_type=F32)
-            scaled = normed_grad * root_scale * gain
-            key_grad = inverse * scaled - key_pre * (inverse * inverse * inverse) * jnp.mean(
-                scaled * key_pre, axis=-1, keepdims=True
-            )
-            gs[hh, 0, slot] = key_grad.astype(BF)
-            gs[hh, 1, slot] = value_grad.astype(BF)
-            return carry
-
-        lax.fori_loop(0, 2, body, 0)
-        pair = pl.ds(2 * mg, 2)
-        for step in (1, 3, 0):
+        micro = (px + OFFSETS[slot]) % NX
+        key_pre = rk[hh, 0, 0, slot].astype(F32)
+        value = rk[hh, 1, 0, slot].astype(F32)
+        for step in (1, 2):
+            key_pre += rk[hh, 0, step, slot].astype(F32)
+            value += rk[hh, 1, step, slot].astype(F32)
+        value = value.astype(BF)
+        inverse = lax.rsqrt(
+            jnp.mean(key_pre * key_pre, axis=-1, keepdims=True) + EPSILON
+        )
+        key = (key_pre * inverse * gain).astype(BF)
+        slots = lax.broadcasted_iota(jnp.int32, (ROWS, 2 * ROWS), 0)
+        texts = lax.broadcasted_iota(jnp.int32, (ROWS, 2 * ROWS), 1) % ROWS
+        first = tiles[0, 0, micro] * TILE_TOK
+        second = first + tiles[0, 1, micro] * TILE_TOK
+        seen = ((slots < first) & (texts >= starts[0, 0, micro])) | (
+            (slots >= first) & (slots < second) & (texts >= starts[0, 1, micro])
+        )
+        visible = jnp.where(seen, 1.0, 0.0).astype(F32)
+        value_grad = jnp.zeros((ROWS, HD), F32)
+        normed_grad = jnp.zeros((ROWS, HD), F32)
+        for g in range(0, GROUPS, 2):
+            low = (hh * GROUPS + g) * HD
+            query = jnp.concatenate(
+                [qb[slot, :, low : low + HD], qb[slot, :, low + HD : low + 2 * HD]], axis=0
+            )
+            grad = jnp.concatenate(
+                [do[slot, :, low : low + HD], do[slot, :, low + HD : low + 2 * HD]], axis=0
+            )
+            scores = (
+                lax.dot_general(key, query, NT, preferred_element_type=F32) * root_scale
+            )
+            weights = jnp.exp(scores) * visible
+            total = jnp.sum(weights, axis=0, keepdims=True)
+            probability = weights * (1.0 / jnp.where(total > 0, total, 1.0))
+            prob_grad = lax.dot_general(value, grad, NT, preferred_element_type=F32)
+            delta = jnp.sum(probability * prob_grad, axis=0, keepdims=True)
+            score_grad = (probability * (prob_grad - delta)).astype(BF)
+            value_grad += jnp.dot(
+                probability.astype(BF), grad, preferred_element_type=F32
+            )
+            normed_grad += jnp.dot(score_grad, query, preferred_element_type=F32)
+        scaled = normed_grad * root_scale * gain
+        key_grad = inverse * scaled - key_pre * (inverse * inverse * inverse) * jnp.mean(
+            scaled * key_pre, axis=-1, keepdims=True
+        )
+        gs[hh, 0, slot] = key_grad.astype(BF)
+        gs[hh, 1, slot] = value_grad.astype(BF)
+        for way in (slot % 2, 1 - slot % 2):
             for same in (1, 0):
                 kind = cc if same else oc
-                src = gs.at[hh, kind, pair]
-                dst = ga.at[hh, qy, pair, cc]
-                if step == 0 and same:
-                    local(("g", hh, mg), src, dst).start()
-                else:
-                    send(("g", hh, mg, step, same), src, dst, at_y(step, kind))
-
-    def relay_grads(hh, mg):
-        for step, slot in ((1, 2 * mg), (3, 2 * mg + 1)):
-            source = (qy - step + NY) % NY
-            for same in (1, 0):
-                receive(
-                    ("g", hh, mg, step, same),
-                    ga.at[hh, source, pl.ds(2 * mg, 2), cc if same else oc],
+                send(
+                    ("g", hh, slot, way, same),
+                    gs.at[hh, kind, slot],
+                    ga.at[hh, qy, slot, cc],
+                    at_y(1 if way == RIGHT else 3, kind),
                 )
-            block = ga.at[hh, source, slot]
-            send(("gh", hh, mg, step), block, block, at_y(step, cc))
-
-    def gathered(hh, mg):
-        pair = pl.ds(2 * mg, 2)
-        dst = ga.at[hh, qy, pair, cc]
-        local(("g", hh, mg), dst, dst).wait()
-        receive(("g", hh, mg, 0, 0), ga.at[hh, qy, pair, oc])
-        for step, slot in ((1, 2 * mg), (3, 2 * mg + 1)):
-            receive(("gh", hh, mg, step), ga.at[hh, (qy + 2) % NY, slot])
+        send(("g", hh, slot), gs.at[hh, oc, slot], ga.at[hh, qy, slot, cc], sibling)
+        local(("lg", hh, slot), gs.at[hh, cc, slot], ga.at[hh, qy, slot, cc]).start()
+
+    def near_grads(hh, slot, way):
+        source = (qy + (3 if way == RIGHT else 1)) % NY
+        for same in (1, 0):
+            receive(("g", hh, slot, way, same), ga.at[hh, source, slot, cc if same else oc])
+        return source
+
+    def relay_grads(hh, slot):
+        way = slot % 2
+        block = ga.at[hh, near_grads(hh, slot, way), slot]
+        send(("gh", hh, slot), block, block, at_y(1 if way == RIGHT else 3, cc))
+
+    def gathered(hh, slot):
+        loaded(("lg", hh, slot), ga.at[hh, qy, slot, cc])
+        receive(("g", hh, slot), ga.at[hh, qy, slot, oc])
+        for way in (RIGHT, LEFT):
+            near_grads(hh, slot, way)
+        receive(("gh", hh, slot), ga.at[hh, (qy + 2) % NY, slot])
 
     def weight_term(hh, distance):
+        for slot in range(NX):
+            gathered(hh, slot)
         block = (zz + distance) % NZ
         lhs = ft[pl.ds(pl.multiple_of(block * 256, 256), 256), :]
 
@@ -399,8 +437,32 @@
 
         lax.fori_loop(0, 2, body, 0)
 
+    def weight_pair(hh, distance):
+        for slot in range(NX):
+            gathered(hh, slot)
+        ends = (distance, NZ - distance)
+
+        def body(n, carry):
+            columns = pl.ds(pl.multiple_of(n * 256, 256), 256)
+            grads = jnp.concatenate(
+                [ga[hh, n * 2 + j].reshape(8 * ROWS, HD) for j in (0, 1)], axis=1
+            )
+            rows = [
+                ft[pl.ds(pl.multiple_of((zz + end) % NZ * 256, 256), 256), :] for end in ends
+            ]
+            total = jnp.dot(
+                jnp.concatenate(rows, axis=0), grads, preferred_element_type=F32
+            )
+            pw[hh, ends[0], :, columns] = total[:256]
+            pw[hh, ends[1], :, columns] = total[256:]
+            return carry
+
+        lax.fori_loop(0, 2, body, 0)
+
     def scatter(hh, n):
         k, second = (n + 1) // 2, n % 2
+        if n == 1:
+            sent(("rs", hh, 0))
         in_flight["rs", hh, n] = copies = []
         for direction in (RIGHT, LEFT):
             piece = 1 - direction if second else direction
@@ -445,7 +507,10 @@
         for j in range(NY):
             ow[cc, hh, j] = own[:, j * HD : (j + 1) * HD]
 
-    def feature_term(hh, pair):
+    def feature_term(hh, pair, part):
+        for slot in (2 * pair, 2 * pair + 1):
+            gathered(hh, slot)
+
         def body(n, carry):
             columns = pl.ds(pl.multiple_of(n * 256, 256), 256)
             grads = jnp.concatenate(
@@ -466,8 +531,8 @@
                     ds[slot, :, columns] = jnp.where(cc == 0, terms[1], terms[0]).astype(BF)
             return carry
 
-        lax.fori_loop(0, NZ, body, 0)
-        if hh == 1:
+        lax.fori_loop(part * HALF, part * HALF + HALF, body, 0)
+        if hh == 1 and part == 1:
             for slot in (2 * pair + 1, 2 * pair):
                 send(("df", slot), ds.at[slot], dr.at[slot], sibling)
 
@@ -486,6 +551,7 @@
 
     def feature_send(way, second):
         slot = 1 if way == RIGHT else 2
+        receive(("df", slot), dr.at[slot])
         low = half * (way if second else 1 - way)
         total = af[slot, 0, low : low + half] + dr[slot, low : low + half].astype(F32)
         if second:
@@ -500,122 +566,123 @@
             at_x(1 if way == RIGHT else 3),
         )
 
-    own_weights(0)
+    def feature_done():
+        receive(("df", 0), dr.at[0])
+        for way in (RIGHT, LEFT):
+            for second in (0, 1):
+                low = half * (way if second else 1 - way)
+                receive(("xr", way, second), xr.at[way, pl.ds(low, half)])
+        total = af[0, 0] + dr[0].astype(F32)
+        for way in (RIGHT, LEFT):
+            total = total + xr[way].astype(F32)
+        dx[0] = total.astype(BF)
+        local("of", dx.at[0], out_f.at[0]).start()
+
+    norm_queries(2)
     gather(0, 0)
+    norm_queries(3)
+    transpose_features(0, 0)
+    transpose_features(0, 1)
+    gather(0, 1)
     norm_queries(0)
-    sent(("ag", 0, 0))
-    gather(0, 1)
+    gather(0, 2)
     norm_queries(1)
-    gather(0, 2)
-    norm_queries(2)
     gather(0, 3)
-    norm_queries(3)
-    local("f", fa.at[0, cc], fa.at[0, cc]).wait()
-    transpose_features(0, cc)
+    relay_features(1)
+    relay_features(0)
+    transpose_features(2, 1)
     gather(0, 4)
-    receive(("fs", 0), fa.at[0, oc])
-    transpose_features(0, oc)
+    transpose_features(1, 1)
     gather(0, 5)
-    receive(("fx", 1), fa.at[1, cc])
-    send(("fh", 0), fa.at[1, cc, pl.ds(0, 64)], fa.at[3, cc, pl.ds(0, 64)], at_x(3))
-    receive(("fx", 3), fa.at[2, cc])
-    send(("fh", 1), fa.at[2, cc, pl.ds(64, 64)], fa.at[3, cc, pl.ds(64, 64)], at_x(1))
-    send(("fs", 1), fa.at[1, cc], fa.at[1, cc], sibling)
-    send(("fs", 2), fa.at[2, cc], fa.at[2, cc], sibling)
-    own_weights(1)
+    transpose_features(2, 0)
+    transpose_features(1, 0)
     gather(0, 6)
-    transpose_features(1, cc)
-    transpose_features(2, cc)
-    sent(("ag", 0, 5))
+    transpose_features(3, 1)
     gather(1, 0)
-    receive(("fh", 0), fa.at[3, cc, pl.ds(0, 64)])
-    receive(("fh", 1), fa.at[3, cc, pl.ds(64, 64)])
-    send(("fs", 3), fa.at[3, cc], fa.at[3, cc], sibling)
-    sent(("ag", 0, 6))
+    far_features()
+    transpose_features(3, 0)
     gather(1, 1)
-    gather_done(0)
-    receive(("fs", 1), fa.at[1, oc])
     project(0, 0)
+    near_keys(0, 0, 0)
+    near_keys(0, 0, 1)
     gather(1, 2)
-    receive(("fs", 2), fa.at[2, oc])
-    receive(("fs", 3), fa.at[3, oc])
     project(0, 1)
+    near_keys(0, 1, 0)
     gather(1, 3)
-    transpose_features(1, oc)
-    relay_keys(0, 0)
-    transpose_features(2, oc)
-    relay_keys(0, 1)
+    near_keys(0, 1, 1)
+    relay_keys(0, 0, 1)
+    relay_keys(0, 0, 0)
     gather(1, 4)
-    transpose_features(3, cc)
-    transpose_features(3, oc)
-    for slot in range(NX):
-        local(("d", slot), do.at[slot], do.at[slot]).wait()
-    projected(0, 0)
+    relay_keys(0, 1, 0)
+    relay_keys(0, 1, 1)
+    gather(1, 5)
     attend(0, 0)
-    gather(1, 5)
-    projected(0, 1)
+    attend(0, 2)
+    gather(1, 6)
     attend(0, 1)
-    gather(1, 6)
     relay_grads(0, 0)
+    attend(0, 3)
+    relay_grads(0, 2)
     relay_grads(0, 1)
-    gather_done(1)
+    project(1, 1)
+    relay_grads(0, 3)
     project(1, 0)
-    project(1, 1)
-    gathered(0, 0)
-    gathered(0, 1)
+    feature_term(0, 0, 0)
+    near_keys(1, 0, 0)
+    relay_keys(1, 1, 0)
+    relay_keys(1, 1, 1)
+    near_keys(1, 1, 1)
+    near_keys(1, 1, 0)
     weight_term(0, 4)
     scatter(0, 0)
-    weight_term(0, 3)
-    weight_term(0, 5)
-    sent(("rs", 0, 0))
+    relay_keys(1, 0, 1)
+    weight_pair(0, 3)
+    feature_term(0, 0, 1)
+    near_keys(1, 0, 1)
+    relay_keys(1, 0, 0)
     scatter(0, 1)
-    relay_keys(1, 0)
-    relay_keys(1, 1)
-    weight_term(0, 2)
-    weight_term(0, 6)
+    attend(1, 2)
     scatter(0, 2)
-    for distance in (1, 7, 0):
-        weight_term(0, distance)
+    attend(1, 3)
+    weight_pair(0, 2)
+    weight_term(0, 0)
     scatter(0, 3)
-    projected(1, 0)
+    relay_grads(1, 2)
+    attend(1, 1)
+    relay_grads(1, 3)
+    scatter(0, 4)
     attend(1, 0)
-    scatter(0, 4)
-    projected(1, 1)
-    attend(1, 1)
+    weight_pair(0, 1)
+    relay_grads(1, 1)
     scatter(0, 5)
+    feature_term(0, 1, 0)
     relay_grads(1, 0)
-    feature_term(0, 1)
+    feature_term(0, 1, 1)
     scatter(0, 6)
-    relay_grads(1, 1)
-    feature_term(0, 0)
-    gathered(1, 0)
-    gathered(1, 1)
+    feature_term(1, 1, 0)
     weight_term(1, 4)
     scatter(1, 0)
-    weight_term(1, 3)
-    weight_term(1, 5)
+    feature_term(1, 1, 1)
+    weight_term(1, 0)
+    weight_pair(1, 3)
     scatter(1, 1)
-    feature_term(1, 1)
+    feature_term(1, 0, 0)
+    feature_far()
     scatter(1, 2)
-    for distance in (2, 6):
-        weight_term(1, distance)
-    feature_far()
+    feature_term(1, 0, 1)
+    feature_send(1, 0)
+    weight_pair(1, 2)
     scatter(1, 3)
-    receive(("df", 2), dr.at[2])
-    feature_send(LEFT, 0)
-    feature_term(1, 0)
+    scatter_done(0)
+    weight_pair(1, 1)
+    feature_send(0, 0)
     scatter(1, 4)
-    receive(("df", 1), dr.at[1])
-    feature_send(RIGHT, 0)
-    for distance in (1, 7, 0):
-        weight_term(1, distance)
+    feature_send(0, 1)
     scatter(1, 5)
-    feature_send(LEFT, 1)
-    feature_send(RIGHT, 1)
-    scatter_done(0)
-    receive(("df", 0), dr.at[0])
+    feature_send(1, 1)
     scatter(1, 6)
     scatter_done(1)
+    feature_done()
 
     for hh in (0, 1):
         receive(("ow", hh), ow.at[oc, hh])
@@ -627,15 +694,6 @@
                     ow.at[kind, hh, j],
                     out.at[0, :, pl.ds((2 * j + hh) * HD, HD)],
                 ).start()
-    for way in (RIGHT, LEFT):
-        for second in (0, 1):
-            low = half * (way if second else 1 - way)
-            receive(("xr", way, second), xr.at[way, pl.ds(low, half)])
-    total = af[0, 0] + dr[0].astype(F32)
-    for way in (RIGHT, LEFT):
-        total = total + xr[way].astype(F32)
-    dx[0] = total.astype(BF)
-    local("of", dx.at[0], out_f.at[0]).start()
     for kind, out in ((0, out_k), (1, out_v)):
         for hh in (0, 1):
             for j in range(NY):

time: 119 us -> 116 us (0.975)
  Pallas kernels: 118 us -> 115 us
    pallas_call x1, Pallas kernels: 116 us -> 113 us  [per_device(): pl.pallas_call(kernel, out_shape=(jax.ShapeDtypeStruct((1, ROWS, WIDTH),...]
where the time goes in v3:
time: 116 us
  Pallas kernels  115 us (99%)
    pallas_call x1, Pallas kernels, per_device(): pl.pallas_call(kernel, out_shape=(jax.ShapeDtypeStruct((1, ROWS, WIDTH),...  113 us

profile of v3, /device:TPU:1, one launch (start us, length us, event | category | flops | bytes accessed | tf_op | source)
XLA Modules:
  0.0 115.5 jit_solution(5953538518411896696)
XLA Ops:
  0.6 112.7 %cross_attention_backward.1 = (bf16[1,128,2048]{2,1,0:T(8,128)(2,1)}, bf16[1,128,1024]{2,1,0:T(8,128)(2,1)}, bf16[1,128,1024]{2,1,0:T(8,128)(2,1)}) custom-call(bf16[1,4,128,2048]{3,2,1,0:T(8,128)(2,1)} %queries.1, bf16[1,4,128,2048]{3,2,1,0:T(8,128)(2,1)} %grad_out.1, bf16[1,128,2048]{2,1,0:T(8,128)(2,1)} %features.1, bf16[1,128,1024]{2,1,0:T(8,128)(2,1)} %w_key.1, ...), custom_call_target="tpu_custom_call" | custom-call | flops 13958643712 | bytes 8388608 | tf_op jit(solution)/shard_map/cross_attention_backward/pallas_call | solution.py:733
  113.3 2.1 %copy_results.1 = (bf16[1,128,2048]{2,1,0:T(8,128)(2,1)}, bf16[1,128,1024]{2,1,0:T(8,128)(2,1)}, bf16[1,128,1024]{2,1,0:T(8,128)(2,1)}) custom-call(bf16[1,128,2048]{2,1,0:T(8,128)(2,1)} %get-tuple-element.6.a, bf16[1,128,1024]{2,1,0:T(8,128)(2,1)} %get-tuple-element.7.b, bf16[1,128,1024]{2,1,0:T(8,128)(2,1)} %get-tuple-element.8.c), custom_call_target="tpu_custom_call" | custom-call | tf_op jit(solution)/shard_map/copy_results/pallas_call | solution.py:776

commit v4 on v3

--- a/solution.py
+++ b/solution.py
@@ -708,16 +708,12 @@
     assert len(ids) <= N_SEMS and len(local_ids) <= 64, (len(ids), len(local_ids))
 
 
-def copy_results(a, b, c, x, y, z, hold_a, hold_b, hold_c, sems):
-    parts = ((a, hold_a, x), (b, hold_b, y), (c, hold_c, z))
-    reads = [pltpu.make_async_copy(p[0], p[1], sems.at[n]) for n, p in enumerate(parts)]
-    writes = [pltpu.make_async_copy(p[1], p[2], sems.at[3 + n]) for n, p in enumerate(parts)]
-    for copy in reads:
+def copy_results(a, b, c, x, y, z, sems):
+    parts = ((a, x), (b, y), (c, z))
+    copies = [pltpu.make_async_copy(p[0], p[1], sems.at[n]) for n, p in enumerate(parts)]
+    for copy in copies:
         copy.start()
-    for n in range(3):
-        reads[n].wait()
-        writes[n].start()
-    for copy in writes:
+    for copy in copies:
         copy.wait()
 
 
@@ -733,12 +729,12 @@
     results = pl.pallas_call(
         kernel,
         out_shape=(
-            jax.ShapeDtypeStruct((1, ROWS, WIDTH), BF),
-            jax.ShapeDtypeStruct((1, ROWS, 1024), BF),
-            jax.ShapeDtypeStruct((1, ROWS, 1024), BF),
+            pltpu.VMEM((1, ROWS, WIDTH), BF),
+            pltpu.VMEM((1, ROWS, 1024), BF),
+            pltpu.VMEM((1, ROWS, 1024), BF),
         ),
         in_specs=[hbm, hbm, hbm, hbm, hbm, vmem, vmem, smem, smem],
-        out_specs=(hbm, hbm, hbm),
+        out_specs=(vmem, vmem, vmem),
         scratch_shapes=[
             pltpu.VMEM((4, ROWS, WIDTH), BF),
             pltpu.VMEM((4, ROWS, WIDTH), BF),
@@ -773,15 +769,15 @@
         ),
         name="cross_attention_backward",
     )(queries, grad_out, features, w_key, w_value, q_gain, k_gain, tiles, starts)
+    held = [pltpu.with_memory_space_constraint(r, pltpu.VMEM) for r in results]
     return pl.pallas_call(
         copy_results,
         out_shape=tuple(jax.ShapeDtypeStruct(r.shape, r.dtype) for r in results),
-        in_specs=[hbm, hbm, hbm],
+        in_specs=[vmem, vmem, vmem],
         out_specs=(hbm, hbm, hbm),
-        scratch_shapes=[pltpu.VMEM(r.shape, r.dtype) for r in results]
-        + [pltpu.SemaphoreType.DMA((6,))],
+        scratch_shapes=[pltpu.SemaphoreType.DMA((3,))],
         name="copy_results",
-    )(*results)
+    )(*held)
 
 
 def solution(mesh):

time: 116 us -> 114 us (0.983)
  Pallas kernels: 115 us -> 113 us
where the time goes in v4:
time: 114 us
  Pallas kernels  113 us (99%)
    pallas_call x1, Pallas kernels, per_device(): pl.pallas_call(kernel, out_shape=(pltpu.VMEM((1, ROWS, WIDTH), BF), pltpu...  112 us

profile of v4, /device:TPU:1, one launch (start us, length us, event | category | flops | bytes accessed | tf_op | source)
XLA Modules:
  0.0 113.8 jit_solution(4798130474978982622)
XLA Ops:
  0.6 112.0 %cross_attention_backward.1 = (bf16[1,128,2048]{2,1,0:T(8,128)(2,1)S(1)}, bf16[1,128,1024]{2,1,0:T(8,128)(2,1)S(1)}, bf16[1,128,1024]{2,1,0:T(8,128)(2,1)S(1)}) custom-call(bf16[1,4,128,2048]{3,2,1,0:T(8,128)(2,1)} %queries.1, bf16[1,4,128,2048]{3,2,1,0:T(8,128)(2,1)} %grad_out.1, bf16[1,128,2048]{2,1,0:T(8,128)(2,1)} %features.1, ...), custom_call_target="tpu_custom_call" | custom-call | flops 13958643712 | bytes 8388608 | tf_op jit(solution)/shard_map/cross_attention_backward/pallas_call | solution.py:729
  112.7 1.0 copy_results.1
